TPU v7x, 32 devices: a whole 2x2x4 slice. The times are simulated.
32 devices in a mesh: row: 4 (over y, x), col: 8 (over z, core).
Axes of the slice: x: 2, y: 2, z: 4, core: 2. Of those that a mesh axis runs over, the one named last changes fastest.
Arguments:
- unfolding: float32 [1024, 4096], P('row', 'col'), may hold values from -40 to 40, as said below
- factor: float32 [1024, 64], replicated, may hold values from -6 to 6
Outputs:
- gram_lower: float32 [1024, 1024], P(('row', 'col'))
- new_factor: float32 [1024, 64], replicated
- core: float32 [64, 4096], P('row', 'col')
Inputs may be any that keep to these rules, and one draw needn't show every extreme that they name: Entries of the unfolding are real values.
All inputs are finite; a program needn't handle non-finite values.
Results may differ from a plain program's by a relative error of at most 0.0003.
Values sent between devices are 32-bit elements; how exact they have to be, the bound alone decides.
No kernel may reach another device: no remote copies, remote signals or barrier semaphores. Data moves between devices by JAX's collectives and lax.ppermute only.
A program may use at most 64 MiB of HBM per device.

v0:
```python
import functools
import math

import jax
import jax.numpy as jnp
from jax import lax
from jax.experimental import pallas as pl
from jax.experimental.pallas import tpu as pltpu
from jax.sharding import PartitionSpec as P

F32 = jnp.float32
BF16 = jnp.bfloat16
NN = ((1,), (0,))
NT = ((1,), (1,))


COST = dict(project=10**6, term=10**10, finish=10**6, gram=10**6, pieces=10**6, unpack=10**6)


def tree_sum(parts):
    while len(parts) > 1:
        paired = [a + b for a, b in zip(parts[::2], parts[1::2])]
        parts = paired + parts[2 * len(paired) :]
    return parts[0]


def split2(a):
    hi = a.astype(BF16)
    return hi, (a - hi.astype(F32)).astype(BF16)


def split3(a):
    hi = a.astype(BF16)
    rest = a - hi.astype(F32)
    mid = rest.astype(BF16)
    return hi, mid, (rest - mid.astype(F32)).astype(BF16)


def mm(a, b, dims):
    return lax.dot_general(a, b, (dims, ((), ())), preferred_element_type=F32)


def mm3(a, b, dims):
    return mm(a[1], b[0], dims) + mm(a[0], b[1], dims) + mm(a[0], b[0], dims)


def mm6(a, b, dims):
    low = mm(a[1], b[1], dims) + (mm(a[2], b[0], dims) + mm(a[0], b[2], dims))
    return (low + (mm(a[1], b[0], dims) + mm(a[0], b[1], dims))) + mm(a[0], b[0], dims)


def call(kernel, out_shape, *args, scratch=(), work=1000, name=None):
    return pl.pallas_call(
        kernel,
        out_shape=out_shape,
        in_specs=[pl.BlockSpec(memory_space=pltpu.VMEM)] * len(args),
        out_specs=jax.tree.map(lambda _: pl.BlockSpec(memory_space=pltpu.VMEM), out_shape),
        scratch_shapes=list(scratch),
        compiler_params=pltpu.CompilerParams(vmem_limit_bytes=48 * 2**20),
        cost_estimate=pl.CostEstimate(flops=work, bytes_accessed=0, transcendentals=0),
        name=name,
    )(*args)


def project_kernel(rows_here, factor_ref, x_ref, y_ref):
    row = lax.axis_index("row")
    n_row = factor_ref.shape[1] // rows_here
    mine = factor_ref[:, :rows_here]
    for r in range(1, n_row):
        mine = jnp.where(row == r, factor_ref[:, r * rows_here : (r + 1) * rows_here], mine)
    y_ref[...] = mm3(split2(mine), split2(x_ref[...]), NN)


def term_kernel(scale, x_ref, mine_ref, got_ref, kept_ref, given_ref):
    core = lax.axis_index("col") % 2
    y = mine_ref[...] + got_ref[...]
    term = mm3(split2(y), split2(x_ref[...]), NT) * scale
    hr = term.shape[0] // 2
    kept_ref[...] = jnp.where(core == 0, term[:hr], term[hr:])
    given_ref[...] = jnp.where(core == 0, term[hr:], term[:hr])


def inverse_factor(inner):
    n = inner.shape[0]
    wide = -(-2 * n // 128) * 128
    r = lax.broadcasted_iota(jnp.int32, (n, wide), 0)
    c = lax.broadcasted_iota(jnp.int32, (n, wide), 1)
    w = jnp.where(c == r + n, F32(1.0), F32(0.0))
    w = w + jnp.concatenate([inner, jnp.zeros((n, wide - n), F32)], 1)
    w = [w[8 * i : 8 * i + 8] for i in range(n // 8)]
    sub = lax.broadcasted_iota(jnp.int32, (8, wide), 0)
    done = []
    for b in range(n // 8):
        cols = {
            j: [jnp.broadcast_to(w[i][:, 8 * b + j : 8 * b + j + 1], (8, wide)) for i in range(b, n // 8)]
            for j in range(8)
        }
        for k in range(8):
            pivot = jnp.broadcast_to(cols[k][0][k : k + 1], (8, wide))
            rs = lax.rsqrt(pivot)
            rs = rs * (1.5 - 0.5 * pivot * rs * rs)
            inv = rs * rs
            row = jnp.broadcast_to(w[b][k : k + 1], (8, wide))
            done.append(row[:1] * rs[:1])
            m = [a * inv for a in cols[k]]
            m[0] = jnp.where(sub > k, m[0], F32(0.0))
            for i in range(b, n // 8):
                w[i] = w[i] - m[i - b] * row
            for j in range(k + 1, 8):
                at = jnp.broadcast_to(cols[j][0][k : k + 1], (8, wide))
                cols[j] = [a - f * at for a, f in zip(cols[j], m)]
    return jnp.concatenate(done, 0)[:, n : 2 * n]


def finish_kernel(n_row, counts, mine_ref, other_ref, *refs):
    total = sum(counts)
    pieces, (nf_ref, core_ref, rows_ref) = refs[:total], refs[total:]
    row = lax.axis_index("row")
    core = lax.axis_index("col") % 2
    _, hr, rows_here = mine_ref.shape
    rank = 2 * hr
    mode = rows_here * n_row
    blocks = []
    for s in range(n_row):
        mine, other = mine_ref[s], other_ref[s]
        first, second = jnp.where(core == 0, mine, other), jnp.where(core == 0, other, mine)
        blocks.append(jnp.concatenate([first, second], 0))
    split = [split3(b) for b in blocks]
    inner = tree_sum([mm6(s, s, NT) for s in split]) * (1.0 / mode)
    inv = inverse_factor(inner)
    z, at = [], 0
    for s in range(n_row):
        start = 0
        for _ in range(counts[s]):
            x = pieces[at][...]
            hi, lo = split[s][0], split[s][1]
            stop = start + x.shape[0]
            z.append(mm3((hi[:, start:stop], lo[:, start:stop]), split2(x), NN))
            start, at = stop, at + 1
    z = tree_sum(z)
    rank_here = rank // n_row
    for i in range(n_row):
        rows_ref[i] = inv[i * rank_here : (i + 1) * rank_here]
    core_ref[...] = mm6(split3(rows_ref[row]), split3(z), NN) * (1.0 / math.sqrt(mode))
    inv3 = split3(inv)
    for s in range(n_row):
        block = mm6(inv3, split[s], NN)
        if len(nf_ref.shape) == 3:
            nf_ref[row ^ s] = block
        else:
            nf_ref[:, pl.ds(pl.multiple_of((row ^ s) * rows_here, rows_here), rows_here)] = block


def gram_kernel(n_row, n_col, scale, counts, *refs):
    total = sum(counts)
    pieces, (given_ref, kept_ref, hi_ref, lo_ref, part_ref) = refs[:total], refs[total:]
    row = lax.axis_index("row")
    core = lax.axis_index("col") % 2
    n_z = n_col // 2
    rows_here = hi_ref.shape[1] * 2
    group = rows_here // 2
    half = group // n_col
    at = 0
    for s in range(n_row):
        hi, lo = [], []
        for _ in range(counts[s]):
            h, l = split2(pieces[at][...])
            hi.append(h)
            lo.append(l)
            at += 1
        hi, lo = jnp.concatenate(hi, 0), jnp.concatenate(lo, 0)
        owner = row ^ s
        for i in range(2):
            hi_ref[2 * owner + i] = hi[i * group : (i + 1) * group]
            lo_ref[2 * owner + i] = lo[i * group : (i + 1) * group]
    high = 2 * n_row - 1 - row
    left = (
        jnp.concatenate([hi_ref[high], hi_ref[row]], 0),
        jnp.concatenate([lo_ref[high], lo_ref[row]], 0),
    )
    for r in range(n_row):
        right = (
            jnp.concatenate([hi_ref[2 * r], hi_ref[2 * r + 1]], 0),
            jnp.concatenate([lo_ref[2 * r], lo_ref[2 * r + 1]], 0),
        )
        g = mm3(left, right, NT) * scale
        for i in range(2):
            for h in range(2):
                for p in range(n_col):
                    start = h * group + p * half
                    part_ref[h, 2 * r + i, p] = g[start : start + half, i * group : (i + 1) * group]
    n_high = 2 * n_row - row
    for b in range(2 * n_row + 1):
        is_low = (b >= n_high).astype(jnp.int32)
        block = b - is_low * n_high
        for zz in range(n_z):
            for ref, k in ((given_ref, 1 - core), (kept_ref, core)):
                owner = 2 * zz + k
                piece = jnp.where(is_low == 1, owner, n_col - 1 - owner)
                ref[zz, :, b * group : (b + 1) * group] = part_ref[is_low, block, piece]


def pieces_kernel(n_z, kept_ref, got_ref, keep_ref, give_ref):
    z = lax.axis_index("col") // 2
    for t in range(n_z):
        ref = give_ref if t % 2 else keep_ref
        ref[t // 2] = kept_ref[z ^ t] + got_ref[z ^ t]


def unpack_kernel(n_row, n_col, *refs):
    out_ref = refs[-1]
    row = lax.axis_index("row")
    owner = row * n_col + lax.axis_index("col")
    total = tree_sum([r[0] for r in refs[:-1]])
    half, width = total.shape
    mode = out_ref.shape[1]
    group = width - mode
    r = lax.broadcasted_iota(jnp.int32, (half, mode), 0)
    c = lax.broadcasted_iota(jnp.int32, (half, mode), 1)
    out_ref[half:, :] = jnp.where(c <= mode - (owner + 1) * half + r, total[:, :mode], F32(0.0))
    out_ref[:half, :] = jnp.zeros((half, mode), F32)
    for k in range(n_row):

        @pl.when(row == k)
        def _():
            start, stop = mode - k * group, mode + group
            keep = c[:, : stop - start] <= owner * half + r[:, : stop - start]
            out_ref[:half, : stop - start] = jnp.where(keep, total[:, start:stop], F32(0.0))


def body(unfolding, factor):
    n_row = lax.axis_size("row")
    n_col = lax.axis_size("col")
    n_z = n_col // 2
    rows_here, cols_here = unfolding.shape
    mode = rows_here * n_row
    rank = factor.shape[1]
    hr = rank // 2
    scale = 1.0 / (cols_here * n_col)
    group = rows_here // 2
    half = group // n_col
    width = mode + group

    def over_row(x, s):
        return lax.ppermute(x, "row", [(i, i ^ s) for i in range(n_row)])

    def over_col(x, s):
        return lax.ppermute(x, "col", [(i, i ^ s) for i in range(n_col)])

    def steps(n):
        return [1 << k for k in range(n.bit_length() - 1)]

    y = call(
        functools.partial(project_kernel, rows_here),
        jax.ShapeDtypeStruct((rank, cols_here), F32),
        factor.T,
        unfolding,
        work=COST["project"],
        name="project",
    )
    for s in steps(n_row)[:-1]:
        y = y + over_row(y, s)
    y_got = over_row(y, n_row // 2)

    if n_row == 4:
        one = over_row(unfolding, 1)
        two = over_row(unfolding, 2)
        top = over_row(one[:group], 2)
        bottom = over_row(two[group:], 1)
        blocks = [[unfolding], [one], [two], [top, bottom]]
    else:
        blocks = [[unfolding]] + [[over_row(unfolding, s)] for s in range(1, n_row)]
    counts = tuple(len(b) for b in blocks)
    blocks = [p for b in blocks for p in b]

    kept, given = call(
        functools.partial(term_kernel, scale),
        (jax.ShapeDtypeStruct((hr, rows_here), F32),) * 2,
        unfolding,
        y,
        y_got,
        work=COST["term"],
        name="term",
    )
    image = kept + over_col(given, 1)
    for s in steps(n_z):
        image = image + over_col(image, 2 * s)
    mine = image[None]
    for s in steps(n_row):
        mine = jnp.concatenate([mine, over_row(mine, s)], 0)
    other = over_col(mine, 1)

    rank_here = rank // n_row
    whole = rows_here % 128 == 0
    nf, core_out = call(
        functools.partial(finish_kernel, n_row, counts),
        (
            jax.ShapeDtypeStruct((rank, mode) if whole else (n_row, rank, rows_here), F32),
            jax.ShapeDtypeStruct((rank_here, cols_here), F32),
        ),
        mine,
        other,
        *blocks,
        scratch=[pltpu.VMEM((n_row, rank_here, rank), F32)],
        work=COST["finish"],
        name="finish",
    )
    new_factor = nf.T if whole else nf.transpose(0, 2, 1).reshape(mode, rank)

    given, kept = call(
        functools.partial(gram_kernel, n_row, n_col, scale, counts),
        (jax.ShapeDtypeStruct((n_z, half, width), F32),) * 2,
        *blocks,
        scratch=[
            pltpu.VMEM((2 * n_row, group, cols_here), BF16),
            pltpu.VMEM((2 * n_row, group, cols_here), BF16),
            pltpu.VMEM((2, 2 * n_row, n_col, half, group), F32),
        ],
        work=COST["gram"],
        name="gram",
    )
    keep, give = call(
        functools.partial(pieces_kernel, n_z),
        (jax.ShapeDtypeStruct((n_z // 2, half, width), F32),) * 2,
        kept,
        over_col(given, 1),
        work=COST["pieces"],
        name="pieces",
    )
    got = over_col(give, 2)
    for s in steps(n_z)[1:]:
        keep, give = keep[0::2] + got[0::2], keep[1::2] + got[1::2]
        got = over_col(give, 2 * s)
    gram_lower = call(
        functools.partial(unpack_kernel, n_row, n_col),
        jax.ShapeDtypeStruct((2 * half, mode), F32),
        keep,
        got,
        work=COST["unpack"],
        name="unpack",
    )
    return gram_lower, new_factor, core_out


def solution(mesh):
    in_specs = (P("row", "col"), P())
    out_specs = (P(("row", "col"), None), P(), P("row", "col"))
    return jax.shard_map(body, mesh=mesh, in_specs=in_specs, out_specs=out_specs, check_vma=False)
```

profile of v0, /device:TPU:0, one launch (start us, length us, event | category | flops | bytes accessed | tf_op | source)
XLA Modules:
  0.0 54.0 jit_solution(2612374203860251008)
XLA Ops:
  0.6 3.0 %collective-permute-start = (f32[256,512]{1,0:T(8,128)}, f32[256,512]{1,0:T(8,128)S(1)}, u32[]{:S(2)}, u32[]{:S(2)}) collective-permute-start(f32[256,512]{1,0:T(8,128)} %refs_0_.3), channel_id=1, source_target_pairs={{0,8},{8,0},{16,24},{24,16},{1,9},{9,1},{17,25},{25,17},{2,10},{10... | collective-permute-start | bytes 1572872 | tf_op jit(solution)/shard_map/ppermute | solution.py:245
  3.6 1.5 %collective-permute-start.1 = (f32[256,512]{1,0:T(8,128)}, f32[256,512]{1,0:T(8,128)S(1)}, u32[]{:S(2)}, u32[]{:S(2)}) collective-permute-start(f32[256,512]{1,0:T(8,128)} %refs_0_.3), channel_id=1, source_target_pairs={{0,16},{8,24},{16,0},{24,8},{1,17},{9,25},{17,1},{25,9},{2,18},{10... | collective-permute-start | bytes 1572872 | tf_op jit(solution)/shard_map/ppermute | solution.py:245
  5.2 1.1 %copy-done = f32[256,512]{1,0:T(8,128)S(1)} copy-done((f32[256,512]{1,0:T(8,128)S(1)}, f32[256,512]{1,0:T(8,128)}, u32[]{:S(2)}) %copy-start) | copy-done | bytes 524312
  6.2 0.9 %copy-done.2 = f32[1024,64]{0,1:T(8,128)S(1)} copy-done((f32[1024,64]{0,1:T(8,128)S(1)}, f32[1024,64]{0,1:T(8,128)}, u32[]{:S(2)}) %copy-start.2) | copy-done | bytes 262168
  7.2 0.3 project.1
  7.5 0.6 %collective-permute-start.7 = (f32[64,512]{1,0:T(8,128)S(1)}, f32[64,512]{1,0:T(8,128)S(1)}, u32[]{:S(2)}, u32[]{:S(2)}) collective-permute-start(f32[64,512]{1,0:T(8,128)S(1)} %project.1), channel_id=1, source_target_pairs={{0,8},{8,0},{16,24},{24,16},{1,9},{9,1},{17,25},{25,17},{2,10},{10... | collective-permute-start | bytes 393224 | tf_op jit(solution)/shard_map/ppermute | solution.py:245
  8.1 10.5 %collective-permute-done.7 = f32[64,512]{1,0:T(8,128)S(1)} collective-permute-done((f32[64,512]{1,0:T(8,128)S(1)}, f32[64,512]{1,0:T(8,128)S(1)}, u32[]{:S(2)}, u32[]{:S(2)}) %collective-permute-start.7) | collective-permute-done | bytes 131104 | tf_op jit(solution)/shard_map/ppermute | solution.py:245
  18.6 1.8 %collective-permute-start.8 = (f32[64,512]{1,0:T(8,128)S(1)}, f32[64,512]{1,0:T(8,128)S(1)}, u32[]{:S(2)}, u32[]{:S(2)}) collective-permute-start(f32[64,512]{1,0:T(8,128)S(1)} %add.20.mine_ref), channel_id=1, source_target_pairs={{0,16},{8,24},{16,0},{24,8},{1,17},{9,25},{17,1},{25,9},{2,18},{10... | collective-permute-start | bytes 393224 | tf_op jit(solution)/shard_map/ppermute | solution.py:245
  20.4 0.0 collective-permute-done.refs_1_
  20.5 0.3 collective-permute-start.2
  20.8 0.0 collective-permute-done.1.refs_2_
  20.8 1.8 %collective-permute-start.3 = (f32[128,512]{1,0:T(8,128)S(1)}, f32[128,512]{1,0:T(8,128)S(1)}, u32[]{:S(2)}, u32[]{:S(2)}) collective-permute-start(f32[128,512]{1,0:T(8,128)S(1)} %slice.29), channel_id=1, source_target_pairs={{0,8},{8,0},{16,24},{24,16},{1,9},{9,1},{17,25},{25,17},{2,10},{10... | collective-permute-start | bytes 786440 | tf_op jit(solution)/shard_map/ppermute | solution.py:245
  22.6 2.5 %collective-permute-done.8.got_ref = f32[64,512]{1,0:T(8,128)S(1)} collective-permute-done((f32[64,512]{1,0:T(8,128)S(1)}, f32[64,512]{1,0:T(8,128)S(1)}, u32[]{:S(2)}, u32[]{:S(2)}) %collective-permute-start.8) | collective-permute-done | bytes 131104 | tf_op jit(solution)/shard_map/ppermute | solution.py:245
  25.1 0.4 term.1
  25.5 0.1 collective-permute-start.9
  25.5 1.2 %collective-permute-done.9 = f32[32,256]{1,0:T(8,128)S(1)} collective-permute-done((f32[32,256]{1,0:T(8,128)S(1)}, f32[32,256]{1,0:T(8,128)S(1)}, u32[]{:S(2)}, u32[]{:S(2)}) %collective-permute-start.9) | collective-permute-done | bytes 32800 | tf_op jit(solution)/shard_map/ppermute | solution.py:248
  26.7 1.8 %collective-permute-start.10 = (f32[32,256]{1,0:T(8,128)S(1)}, f32[32,256]{1,0:T(8,128)S(1)}, u32[]{:S(2)}, u32[]{:S(2)}) collective-permute-start(f32[32,256]{1,0:T(8,128)S(1)} %add.21), channel_id=1, source_target_pairs={{0,2},{1,3},{2,0},{3,1},{4,6},{5,7},{6,4},{7,5},{8,10},{9,11},{10,... | collective-permute-start | bytes 98312 | tf_op jit(solution)/shard_map/ppermute | solution.py:248
  28.6 2.1 %collective-permute-done.10 = f32[32,256]{1,0:T(8,128)S(1)} collective-permute-done((f32[32,256]{1,0:T(8,128)S(1)}, f32[32,256]{1,0:T(8,128)S(1)}, u32[]{:S(2)}, u32[]{:S(2)}) %collective-permute-start.10) | collective-permute-done | bytes 32800 | tf_op jit(solution)/shard_map/ppermute | solution.py:248
  30.7 2.8 %collective-permute-start.11 = (f32[32,256]{1,0:T(8,128)S(1)}, f32[32,256]{1,0:T(8,128)S(1)}, u32[]{:S(2)}, u32[]{:S(2)}) collective-permute-start(f32[32,256]{1,0:T(8,128)S(1)} %add.22), channel_id=1, source_target_pairs={{0,4},{1,5},{2,6},{3,7},{4,0},{5,1},{6,2},{7,3},{8,12},{9,13},{10,... | collective-permute-start | bytes 98312 | tf_op jit(solution)/shard_map/ppermute | solution.py:248
  33.5 1.6 %gram.1 = (f32[4,16,1152]{2,1,0:T(8,128)S(1)}, f32[4,16,1152]{2,1,0:T(8,128)S(1)}) custom-call(f32[256,512]{1,0:T(8,128)S(1)} %copy-done, f32[256,512]{1,0:T(8,128)S(1)} %collective-permute-done.refs_1_, f32[256,512]{1,0:T(8,128)S(1)} %collective-permute-done.1.refs_2_, f32[128,512]{1,0:T(8,128)S(1)} %collective-permute-done.2.refs_3_, ...), custom_call_target="tpu_custom_call" | custom-call | flops 1000000 | tf_op jit(solution)/shard_map/gram/pallas_call | solution.py:53
  35.1 0.1 collective-permute-start.4
  35.2 0.3 collective-permute-done.11
  35.5 1.7 %collective-permute-start.12 = (f32[1,32,256]{2,1,0:T(8,128)S(1)}, f32[1,32,256]{2,1,0:T(8,128)S(1)}, u32[]{:S(2)}, u32[]{:S(2)}) collective-permute-start(f32[1,32,256]{2,1,0:T(8,128)S(1)} %add_bitcast_fusion), channel_id=1, source_target_pairs={{0,8},{8,0},{16,24},{24,16},{1,9},{9,1},{17,25},{25,17},{2,10},{10... | collective-permute-start | bytes 98312 | tf_op jit(solution)/shard_map/ppermute | solution.py:245
  37.2 2.2 %collective-permute-done.12 = f32[1,32,256]{2,1,0:T(8,128)S(1)} collective-permute-done((f32[1,32,256]{2,1,0:T(8,128)S(1)}, f32[1,32,256]{2,1,0:T(8,128)S(1)}, u32[]{:S(2)}, u32[]{:S(2)}) %collective-permute-start.12) | collective-permute-done | bytes 32800 | tf_op jit(solution)/shard_map/ppermute | solution.py:245
  39.4 1.8 %collective-permute-start.13 = (f32[2,32,256]{2,1,0:T(8,128)S(1)}, f32[2,32,256]{2,1,0:T(8,128)S(1)}, u32[]{:S(2)}, u32[]{:S(2)}) collective-permute-start(f32[2,32,256]{2,1,0:T(8,128)S(1)} %pad_maximum_fusion.1), channel_id=1, source_target_pairs={{0,16},{8,24},{16,0},{24,8},{1,17},{9,25},{17,1},{25,9},{2,18},{10... | collective-permute-start | bytes 196616 | tf_op jit(solution)/shard_map/ppermute | solution.py:245
  41.2 1.6 %collective-permute-start.5 = (f32[2,16,1152]{2,1,0:T(8,128)S(1)}, f32[2,16,1152]{2,1,0:T(8,128)S(1)}, u32[]{:S(2)}, u32[]{:S(2)}) collective-permute-start(f32[2,16,1152]{2,1,0:T(8,128)S(1)} %get-tuple-element.14), channel_id=1, source_target_pairs={{0,2},{1,3},{2,0},{3,1},{4,6},{5,7},{6,4},{7,5},{8,10},{9,11},{10,... | collective-permute-start | bytes 442376 | tf_op jit(solution)/shard_map/ppermute | solution.py:248
  42.9 0.8 %collective-permute-done.13 = f32[2,32,256]{2,1,0:T(8,128)S(1)} collective-permute-done((f32[2,32,256]{2,1,0:T(8,128)S(1)}, f32[2,32,256]{2,1,0:T(8,128)S(1)}, u32[]{:S(2)}, u32[]{:S(2)}) %collective-permute-start.13) | collective-permute-done | bytes 65568 | tf_op jit(solution)/shard_map/ppermute | solution.py:245
  43.7 0.1 collective-permute-start.14
  43.8 2.7 %collective-permute-done.5 = f32[2,16,1152]{2,1,0:T(8,128)S(1)} collective-permute-done((f32[2,16,1152]{2,1,0:T(8,128)S(1)}, f32[2,16,1152]{2,1,0:T(8,128)S(1)}, u32[]{:S(2)}, u32[]{:S(2)}) %collective-permute-start.5) | collective-permute-done | bytes 147488 | tf_op jit(solution)/shard_map/ppermute | solution.py:248
  46.4 2.7 %collective-permute-start.6 = (f32[1,16,1152]{2,1,0:T(8,128)S(1)}, f32[1,16,1152]{2,1,0:T(8,128)S(1)}, u32[]{:S(2)}, u32[]{:S(2)}) collective-permute-start(f32[1,16,1152]{2,1,0:T(8,128)S(1)} %get-tuple-element.19), channel_id=1, source_target_pairs={{0,4},{1,5},{2,6},{3,7},{4,0},{5,1},{6,2},{7,3},{8,12},{9,13},{10,... | collective-permute-start | bytes 221192 | tf_op jit(solution)/shard_map/ppermute | solution.py:248
  49.1 4.2 %finish.1 = (f32[64,1024]{1,0:T(8,128)}, f32[16,512]{1,0:T(8,128)}) custom-call(f32[4,32,256]{2,1,0:T(8,128)S(1)} %pad_maximum_fusion.mine_ref, f32[4,32,256]{2,1,0:T(8,128)S(1)} %collective-permute-done.14.other_ref, f32[256,512]{1,0:T(8,128)S(1)} %copy-done.1, f32[256,512]{1,0:T(8,128)S(1)} %collective-permute-done.refs_1_, ...), custom_call_target="tpu_custom_call" | custom-call | flops 1000000 | tf_op jit(solution)/shard_map/finish/pallas_call | solution.py:53
  53.3 0.7 %unpack.1 = f32[32,1024]{1,0:T(8,128)} custom-call(f32[1,16,1152]{2,1,0:T(8,128)S(1)} %get-tuple-element.20.refs_0_, f32[1,16,1152]{2,1,0:T(8,128)S(1)} %collective-permute-done.6.refs_1_), custom_call_target="tpu_custom_call" | custom-call | flops 1000000 | tf_op jit(solution)/shard_map/unpack/pallas_call | solution.py:53
  (19 shorter events, 0.2 us)
Async XLA Ops:
  0.6 19.8 %collective-permute-start = (f32[256,512]{1,0:T(8,128)}, f32[256,512]{1,0:T(8,128)S(1)}, u32[]{:S(2)}, u32[]{:S(2)}) collective-permute-start(f32[256,512]{1,0:T(8,128)} %refs_0_.3), channel_id=1, source_target_pairs={{0,8},{8,0},{16,24},{24,16},{1,9},{9,1},{17,25},{25,17},{2,10},{10... | collective-permute-start | bytes 1572872 | tf_op jit(solution)/shard_map/ppermute | solution.py:245
  3.6 17.2 %collective-permute-start.1 = (f32[256,512]{1,0:T(8,128)}, f32[256,512]{1,0:T(8,128)S(1)}, u32[]{:S(2)}, u32[]{:S(2)}) collective-permute-start(f32[256,512]{1,0:T(8,128)} %refs_0_.3), channel_id=1, source_target_pairs={{0,16},{8,24},{16,0},{24,8},{1,17},{9,25},{17,1},{25,9},{2,18},{10... | collective-permute-start | bytes 1572872 | tf_op jit(solution)/shard_map/ppermute | solution.py:245
  5.2 1.1 %copy-start = (f32[256,512]{1,0:T(8,128)S(1)}, f32[256,512]{1,0:T(8,128)}, u32[]{:S(2)}) copy-start(f32[256,512]{1,0:T(8,128)} %refs_0_.3) | copy-start | bytes 1572868
  6.2 0.9 %copy-start.2 = (f32[1024,64]{0,1:T(8,128)S(1)}, f32[1024,64]{0,1:T(8,128)}, u32[]{:S(2)}) copy-start(f32[1024,64]{0,1:T(8,128)} %param.3) | copy-start | bytes 786436
  7.5 11.1 %collective-permute-start.7 = (f32[64,512]{1,0:T(8,128)S(1)}, f32[64,512]{1,0:T(8,128)S(1)}, u32[]{:S(2)}, u32[]{:S(2)}) collective-permute-start(f32[64,512]{1,0:T(8,128)S(1)} %project.1), channel_id=1, source_target_pairs={{0,8},{8,0},{16,24},{24,16},{1,9},{9,1},{17,25},{25,17},{2,10},{10... | collective-permute-start | bytes 393224 | tf_op jit(solution)/shard_map/ppermute | solution.py:245
  18.6 6.5 %collective-permute-start.8 = (f32[64,512]{1,0:T(8,128)S(1)}, f32[64,512]{1,0:T(8,128)S(1)}, u32[]{:S(2)}, u32[]{:S(2)}) collective-permute-start(f32[64,512]{1,0:T(8,128)S(1)} %add.20.mine_ref), channel_id=1, source_target_pairs={{0,16},{8,24},{16,0},{24,8},{1,17},{9,25},{17,1},{25,9},{2,18},{10... | collective-permute-start | bytes 393224 | tf_op jit(solution)/shard_map/ppermute | solution.py:245
  20.5 13.0 %collective-permute-start.2 = (f32[128,512]{1,0:T(8,128)S(1)}, f32[128,512]{1,0:T(8,128)S(1)}, u32[]{:S(2)}, u32[]{:S(2)}) collective-permute-start(f32[128,512]{1,0:T(8,128)S(1)} %slice.28), channel_id=1, source_target_pairs={{0,16},{8,24},{16,0},{24,8},{1,17},{9,25},{17,1},{25,9},{2,18},{10... | collective-permute-start | bytes 786440 | tf_op jit(solution)/shard_map/ppermute | solution.py:245
  20.8 12.7 %collective-permute-start.3 = (f32[128,512]{1,0:T(8,128)S(1)}, f32[128,512]{1,0:T(8,128)S(1)}, u32[]{:S(2)}, u32[]{:S(2)}) collective-permute-start(f32[128,512]{1,0:T(8,128)S(1)} %slice.29), channel_id=1, source_target_pairs={{0,8},{8,0},{16,24},{24,16},{1,9},{9,1},{17,25},{25,17},{2,10},{10... | collective-permute-start | bytes 786440 | tf_op jit(solution)/shard_map/ppermute | solution.py:245
  25.5 1.3 %collective-permute-start.9 = (f32[32,256]{1,0:T(8,128)S(1)}, f32[32,256]{1,0:T(8,128)S(1)}, u32[]{:S(2)}, u32[]{:S(2)}) collective-permute-start(f32[32,256]{1,0:T(8,128)S(1)} %get-tuple-element.16), channel_id=1, source_target_pairs={{0,1},{1,0},{2,3},{3,2},{4,5},{5,4},{6,7},{7,6},{8,9},{9,8},{10,11... | collective-permute-start | bytes 98312 | tf_op jit(solution)/shard_map/ppermute | solution.py:248
  26.7 3.9 %collective-permute-start.10 = (f32[32,256]{1,0:T(8,128)S(1)}, f32[32,256]{1,0:T(8,128)S(1)}, u32[]{:S(2)}, u32[]{:S(2)}) collective-permute-start(f32[32,256]{1,0:T(8,128)S(1)} %add.21), channel_id=1, source_target_pairs={{0,2},{1,3},{2,0},{3,1},{4,6},{5,7},{6,4},{7,5},{8,10},{9,11},{10,... | collective-permute-start | bytes 98312 | tf_op jit(solution)/shard_map/ppermute | solution.py:248
  30.7 4.8 %collective-permute-start.11 = (f32[32,256]{1,0:T(8,128)S(1)}, f32[32,256]{1,0:T(8,128)S(1)}, u32[]{:S(2)}, u32[]{:S(2)}) collective-permute-start(f32[32,256]{1,0:T(8,128)S(1)} %add.22), channel_id=1, source_target_pairs={{0,4},{1,5},{2,6},{3,7},{4,0},{5,1},{6,2},{7,3},{8,12},{9,13},{10,... | collective-permute-start | bytes 98312 | tf_op jit(solution)/shard_map/ppermute | solution.py:248
  35.1 6.1 %collective-permute-start.4 = (f32[4,16,1152]{2,1,0:T(8,128)S(1)}, f32[4,16,1152]{2,1,0:T(8,128)S(1)}, u32[]{:S(2)}, u32[]{:S(2)}) collective-permute-start(f32[4,16,1152]{2,1,0:T(8,128)S(1)} %get-tuple-element.12), channel_id=1, source_target_pairs={{0,1},{1,0},{2,3},{3,2},{4,5},{5,4},{6,7},{7,6},{8,9},{9,8},{10,11... | collective-permute-start | bytes 884744 | tf_op jit(solution)/shard_map/ppermute | solution.py:248
  35.5 3.9 %collective-permute-start.12 = (f32[1,32,256]{2,1,0:T(8,128)S(1)}, f32[1,32,256]{2,1,0:T(8,128)S(1)}, u32[]{:S(2)}, u32[]{:S(2)}) collective-permute-start(f32[1,32,256]{2,1,0:T(8,128)S(1)} %add_bitcast_fusion), channel_id=1, source_target_pairs={{0,8},{8,0},{16,24},{24,16},{1,9},{9,1},{17,25},{25,17},{2,10},{10... | collective-permute-start | bytes 98312 | tf_op jit(solution)/shard_map/ppermute | solution.py:245
  39.4 4.3 %collective-permute-start.13 = (f32[2,32,256]{2,1,0:T(8,128)S(1)}, f32[2,32,256]{2,1,0:T(8,128)S(1)}, u32[]{:S(2)}, u32[]{:S(2)}) collective-permute-start(f32[2,32,256]{2,1,0:T(8,128)S(1)} %pad_maximum_fusion.1), channel_id=1, source_target_pairs={{0,16},{8,24},{16,0},{24,8},{1,17},{9,25},{17,1},{25,9},{2,18},{10... | collective-permute-start | bytes 196616 | tf_op jit(solution)/shard_map/ppermute | solution.py:245
  41.2 7.9 %copy-start.1 = (f32[256,512]{1,0:T(8,128)S(1)}, f32[256,512]{1,0:T(8,128)}, u32[]{:S(2)}) copy-start(f32[256,512]{1,0:T(8,128)} %refs_0_.3) | copy-start | bytes 1572868
  41.2 5.2 %collective-permute-start.5 = (f32[2,16,1152]{2,1,0:T(8,128)S(1)}, f32[2,16,1152]{2,1,0:T(8,128)S(1)}, u32[]{:S(2)}, u32[]{:S(2)}) collective-permute-start(f32[2,16,1152]{2,1,0:T(8,128)S(1)} %get-tuple-element.14), channel_id=1, source_target_pairs={{0,2},{1,3},{2,0},{3,1},{4,6},{5,7},{6,4},{7,5},{8,10},{9,11},{10,... | collective-permute-start | bytes 442376 | tf_op jit(solution)/shard_map/ppermute | solution.py:248
  43.7 5.4 %collective-permute-start.14 = (f32[4,32,256]{2,1,0:T(8,128)S(1)}, f32[4,32,256]{2,1,0:T(8,128)S(1)}, u32[]{:S(2)}, u32[]{:S(2)}) collective-permute-start(f32[4,32,256]{2,1,0:T(8,128)S(1)} %pad_maximum_fusion.mine_ref), channel_id=1, source_target_pairs={{0,1},{1,0},{2,3},{3,2},{4,5},{5,4},{6,7},{7,6},{8,9},{9,8},{10,11... | collective-permute-start | bytes 393224 | tf_op jit(solution)/shard_map/ppermute | solution.py:248
  46.4 6.9 %collective-permute-start.6 = (f32[1,16,1152]{2,1,0:T(8,128)S(1)}, f32[1,16,1152]{2,1,0:T(8,128)S(1)}, u32[]{:S(2)}, u32[]{:S(2)}) collective-permute-start(f32[1,16,1152]{2,1,0:T(8,128)S(1)} %get-tuple-element.19), channel_id=1, source_target_pairs={{0,4},{1,5},{2,6},{3,7},{4,0},{5,1},{6,2},{7,3},{8,12},{9,13},{10,... | collective-permute-start | bytes 221192 | tf_op jit(solution)/shard_map/ppermute | solution.py:248
where the time goes:
time: 54.2 us; the launch traced here: 54 us
  waiting for transfers between devices  22.3 us (41%)
  starting transfers between devices  21.8 us (40%)
  Pallas kernels  7.15 us (13%)
  local copies, waits for them, and re-layouts  2.06 us (4%)
  between operations  0.71 us (1%)
    ppermute x8, waiting for transfers between devices, over_row(): return lax.ppermute(x, 'row', [(i, i ^ s) for i in range(n_row)])  16 us
    ppermute x8, starting transfers between devices, over_row(): return lax.ppermute(x, 'row', [(i, i ^ s) for i in range(n_row)])  12.6 us
    ppermute x7, starting transfers between devices, over_col(): return lax.ppermute(x, 'col', [(i, i ^ s) for i in range(n_col)])  9.19 us
    pallas_call x6, Pallas kernels, call(): pl.pallas_call(kernel, out_shape=out_shape, in_specs=[pl.BlockSpec(memory...  7.15 us
    ppermute x7, waiting for transfers between devices, over_col(): return lax.ppermute(x, 'col', [(i, i ^ s) for i in range(n_col)])  6.24 us
    unnamed x6, local copies, waits for them, and re-layouts  2.03 us
  transfers between devices with their start and end apart: 15, of which 8 were waited for; matrix products, arithmetic and copies ran while one was open for 0% of the time, Pallas kernels for 12%

commit v1 on v0

--- a/solution.py
+++ b/solution.py
@@ -14,7 +14,7 @@
 NT = ((1,), (1,))
 
 
-COST = dict(project=10**6, term=10**10, finish=10**6, gram=10**6, pieces=10**6, unpack=10**6)
+COST = dict(project=10**6, join=10**6, term=10**10, finish=10**6, gram=10**6, pieces=10**6, unpack=10**6)
 
 
 def tree_sum(parts):
@@ -49,26 +49,38 @@
     return (low + (mm(a[1], b[0], dims) + mm(a[0], b[1], dims))) + mm(a[0], b[0], dims)
 
 
-def call(kernel, out_shape, *args, scratch=(), work=1000, name=None):
+def call(kernel, out_shape, *args, after=(), scratch=(), work=1000, name=None):
+    n = len(args)
+
+    def run(*refs):
+        kernel(*refs[:n], *refs[n + len(after) :])
+
     return pl.pallas_call(
-        kernel,
+        run,
         out_shape=out_shape,
-        in_specs=[pl.BlockSpec(memory_space=pltpu.VMEM)] * len(args),
+        in_specs=[pl.BlockSpec(memory_space=pltpu.VMEM)] * n + [pl.BlockSpec(memory_space=pl.ANY)] * len(after),
         out_specs=jax.tree.map(lambda _: pl.BlockSpec(memory_space=pltpu.VMEM), out_shape),
         scratch_shapes=list(scratch),
         compiler_params=pltpu.CompilerParams(vmem_limit_bytes=48 * 2**20),
         cost_estimate=pl.CostEstimate(flops=work, bytes_accessed=0, transcendentals=0),
         name=name,
-    )(*args)
-
-
-def project_kernel(rows_here, factor_ref, x_ref, y_ref):
+    )(*args, *after)
+
+
+def project_kernel(rows_here, factor_ref, x_ref, y_ref, *copies):
     row = lax.axis_index("row")
     n_row = factor_ref.shape[1] // rows_here
     mine = factor_ref[:, :rows_here]
     for r in range(1, n_row):
         mine = jnp.where(row == r, factor_ref[:, r * rows_here : (r + 1) * rows_here], mine)
     y_ref[...] = mm3(split2(mine), split2(x_ref[...]), NN)
+    for i, ref in enumerate(copies):
+        ref[...] = x_ref[i * ref.shape[0] : (i + 1) * ref.shape[0], :]
+
+
+def join_kernel(mine_ref, got_ref, x_ref, y_ref, copy_ref):
+    y_ref[...] = mine_ref[...] + got_ref[...]
+    copy_ref[...] = x_ref[...]
 
 
 def term_kernel(scale, x_ref, mine_ref, got_ref, kept_ref, given_ref):
@@ -250,25 +262,34 @@
     def steps(n):
         return [1 << k for k in range(n.bit_length() - 1)]
 
-    y = call(
-        functools.partial(project_kernel, rows_here),
-        jax.ShapeDtypeStruct((rank, cols_here), F32),
-        factor.T,
-        unfolding,
-        work=COST["project"],
-        name="project",
-    )
-    for s in steps(n_row)[:-1]:
-        y = y + over_row(y, s)
-    y_got = over_row(y, n_row // 2)
-
+    y_shape = jax.ShapeDtypeStruct((rank, cols_here), F32)
+    part_shape = jax.ShapeDtypeStruct((group, cols_here), F32)
+    project = functools.partial(project_kernel, rows_here)
     if n_row == 4:
-        one = over_row(unfolding, 1)
-        two = over_row(unfolding, 2)
-        top = over_row(one[:group], 2)
-        bottom = over_row(two[group:], 1)
-        blocks = [[unfolding], [one], [two], [top, bottom]]
+        two_low = over_row(unfolding[group:], 2)
+        y, upper, lower = call(
+            project,
+            (y_shape, part_shape, part_shape),
+            factor.T,
+            unfolding,
+            work=COST["project"],
+            name="project",
+        )
+        got = over_row(y, 1)
+        one_up = over_row(upper, 1)
+        one_low = over_row(lower, 1)
+        y, upper = call(
+            join_kernel, (y_shape, part_shape), y, got, upper, work=COST["join"], name="join"
+        )
+        y_got = over_row(y, 2)
+        two_up = over_row(upper, 2)
+        three = [over_row(one_up, 2), over_row(two_low, 1)]
+        blocks = [[unfolding], [one_up, one_low], [two_up, two_low], three]
     else:
+        (y,) = call(project, (y_shape,), factor.T, unfolding, work=COST["project"], name="project")
+        for s in steps(n_row)[:-1]:
+            y = y + over_row(y, s)
+        y_got = over_row(y, n_row // 2)
         blocks = [[unfolding]] + [[over_row(unfolding, s)] for s in range(1, n_row)]
     counts = tuple(len(b) for b in blocks)
     blocks = [p for b in blocks for p in b]
@@ -316,6 +337,7 @@
             pltpu.VMEM((2 * n_row, group, cols_here), BF16),
             pltpu.VMEM((2, 2 * n_row, n_col, half, group), F32),
         ],
+        after=[image],
         work=COST["gram"],
         name="gram",
     )

time: 54.2 us -> 49.2 us (0.908)
  waiting for transfers between devices: 22.3 us -> 16.1 us
  starting transfers between devices: 21.8 us -> 22.9 us
    ppermute x8 -> x10, waiting for transfers between devices: 16 us -> 8.82 us  [over_row(): return lax.ppermute(x, 'row', [(i, i ^ s) for i in range(n_row)])]
    ppermute x8 -> x10, starting transfers between devices: 12.6 us -> 14.2 us  [over_row(): return lax.ppermute(x, 'row', [(i, i ^ s) for i in range(n_row)])]
    ppermute x7, waiting for transfers between devices: 6.24 us -> 7.32 us  [over_col(): return lax.ppermute(x, 'col', [(i, i ^ s) for i in range(n_col)])]
    pallas_call x6 -> x7, Pallas kernels: 7.15 us -> 7.14 us  [call(): pl.pallas_call(run, out_shape=out_shape, in_specs=[pl.BlockSpec(memory_sp...]
  transfers between devices with their start and end apart: 15 -> 17, of which waited for: 8 -> 8; matrix products, arithmetic and copies ran while one was open for 0% -> 0% of each run, Pallas kernels for 12% -> 9%
where the time goes in v1:
time: 49.2 us; the launch traced here: 49 us
  starting transfers between devices  22.9 us (47%)
  waiting for transfers between devices  16.1 us (33%)
  Pallas kernels  7.14 us (15%)
  local copies, waits for them, and re-layouts  2.01 us (4%)
  between operations  0.75 us (2%)
    ppermute x10, starting transfers between devices, over_row(): return lax.ppermute(x, 'row', [(i, i ^ s) for i in range(n_row)])  14.2 us
    ppermute x10, waiting for transfers between devices, over_row(): return lax.ppermute(x, 'row', [(i, i ^ s) for i in range(n_row)])  8.82 us
    ppermute x7, starting transfers between devices, over_col(): return lax.ppermute(x, 'col', [(i, i ^ s) for i in range(n_col)])  8.7 us
    ppermute x7, waiting for transfers between devices, over_col(): return lax.ppermute(x, 'col', [(i, i ^ s) for i in range(n_col)])  7.32 us
    pallas_call x7, Pallas kernels, call(): pl.pallas_call(run, out_shape=out_shape, in_specs=[pl.BlockSpec(memory_sp...  7.14 us
    unnamed x6, local copies, waits for them, and re-layouts  1.99 us
  transfers between devices with their start and end apart: 17, of which 8 were waited for; matrix products, arithmetic and copies ran while one was open for 0% of the time, Pallas kernels for 9%

profile of v1, /device:TPU:0, one launch (start us, length us, event | category | flops | bytes accessed | tf_op | source)
XLA Modules:
  0.0 49.0 jit_solution(15084677369567963052)
XLA Ops:
  0.6 1.0 %copy-done = f32[256,512]{1,0:T(8,128)S(1)} copy-done((f32[256,512]{1,0:T(8,128)S(1)}, f32[256,512]{1,0:T(8,128)}, u32[]{:S(2)}) %copy-start) | copy-done | bytes 524312
  1.7 0.9 %copy-done.2 = f32[1024,64]{0,1:T(8,128)S(1)} copy-done((f32[1024,64]{0,1:T(8,128)S(1)}, f32[1024,64]{0,1:T(8,128)}, u32[]{:S(2)}) %copy-start.2) | copy-done | bytes 262168
  2.6 0.3 project.1
  2.9 3.0 %collective-permute-start.2 = (f32[64,512]{1,0:T(8,128)S(1)}, f32[64,512]{1,0:T(8,128)S(1)}, u32[]{:S(2)}, u32[]{:S(2)}) collective-permute-start(f32[64,512]{1,0:T(8,128)S(1)} %get-tuple-element.18.refs_0_), channel_id=1, source_target_pairs={{0,8},{8,0},{16,24},{24,16},{1,9},{9,1},{17,25},{25,17},{2,10},{10... | collective-permute-start | bytes 393224 | tf_op jit(solution)/shard_map/ppermute | solution.py:257
  5.9 0.1 collective-permute-start
  6.0 2.0 %collective-permute-start.4 = (f32[128,512]{1,0:T(8,128)S(1)}, f32[128,512]{1,0:T(8,128)S(1)}, u32[]{:S(2)}, u32[]{:S(2)}) collective-permute-start(f32[128,512]{1,0:T(8,128)S(1)} %slice.19), channel_id=1, source_target_pairs={{0,16},{8,24},{16,0},{24,8},{1,17},{9,25},{17,1},{25,9},{2,18},{10... | collective-permute-start | bytes 786440 | tf_op jit(solution)/shard_map/ppermute | solution.py:257
  8.0 2.2 %collective-permute-done.2.refs_1_ = f32[64,512]{1,0:T(8,128)S(1)} collective-permute-done((f32[64,512]{1,0:T(8,128)S(1)}, f32[64,512]{1,0:T(8,128)S(1)}, u32[]{:S(2)}, u32[]{:S(2)}) %collective-permute-start.2) | collective-permute-done | bytes 131104 | tf_op jit(solution)/shard_map/ppermute | solution.py:257
  10.3 2.2 %collective-permute-start.7 = (f32[64,512]{1,0:T(8,128)S(1)}, f32[64,512]{1,0:T(8,128)S(1)}, u32[]{:S(2)}, u32[]{:S(2)}) collective-permute-start(f32[64,512]{1,0:T(8,128)S(1)} %get-tuple-element.20.refs_1_), channel_id=1, source_target_pairs={{0,16},{8,24},{16,0},{24,8},{1,17},{9,25},{17,1},{25,9},{2,18},{10... | collective-permute-start | bytes 393224 | tf_op jit(solution)/shard_map/ppermute | solution.py:257
  12.4 1.5 %collective-permute-start.1 = (f32[128,512]{1,0:T(8,128)S(1)}, f32[128,512]{1,0:T(8,128)S(1)}, u32[]{:S(2)}, u32[]{:S(2)}) collective-permute-start(f32[128,512]{1,0:T(8,128)S(1)} %get-tuple-element.17), channel_id=1, source_target_pairs={{0,8},{8,0},{16,24},{24,16},{1,9},{9,1},{17,25},{25,17},{2,10},{10... | collective-permute-start | bytes 786440 | tf_op jit(solution)/shard_map/ppermute | solution.py:257
  13.9 0.5 %collective-permute-start.3 = (f32[128,512]{1,0:T(8,128)S(1)}, f32[128,512]{1,0:T(8,128)S(1)}, u32[]{:S(2)}, u32[]{:S(2)}) collective-permute-start(f32[128,512]{1,0:T(8,128)S(1)} %get-tuple-element.19), channel_id=1, source_target_pairs={{0,16},{8,24},{16,0},{24,8},{1,17},{9,25},{17,1},{25,9},{2,18},{10... | collective-permute-start | bytes 786440 | tf_op jit(solution)/shard_map/ppermute | solution.py:257
  14.4 1.4 %collective-permute-done.refs_1_.refs_3_ = f32[128,512]{1,0:T(8,128)S(1)} collective-permute-done((f32[128,512]{1,0:T(8,128)S(1)}, f32[128,512]{1,0:T(8,128)S(1)}, u32[]{:S(2)}, u32[]{:S(2)}) %collective-permute-start) | collective-permute-done | bytes 262176 | tf_op jit(solution)/shard_map/ppermute | solution.py:257
  15.8 2.1 %collective-permute-start.5 = (f32[128,512]{1,0:T(8,128)S(1)}, f32[128,512]{1,0:T(8,128)S(1)}, u32[]{:S(2)}, u32[]{:S(2)}) collective-permute-start(f32[128,512]{1,0:T(8,128)S(1)} %collective-permute-done.refs_1_.refs_3_), channel_id=1, source_target_pairs={{0,16},{8,24},{16,0},{24,8},{1,17},{9,25},{17,1},{25,9},{2,18},{10... | collective-permute-start | bytes 786440 | tf_op jit(solution)/shard_map/ppermute | solution.py:257
  17.9 1.5 %collective-permute-start.6 = (f32[128,512]{1,0:T(8,128)S(1)}, f32[128,512]{1,0:T(8,128)S(1)}, u32[]{:S(2)}, u32[]{:S(2)}) collective-permute-start(f32[128,512]{1,0:T(8,128)S(1)} %collective-permute-done.4.refs_4_.refs_6_), channel_id=1, source_target_pairs={{0,8},{8,0},{16,24},{24,16},{1,9},{9,1},{17,25},{25,17},{2,10},{10... | collective-permute-start | bytes 786440 | tf_op jit(solution)/shard_map/ppermute | solution.py:257
  19.4 0.4 term.1
  19.8 0.1 collective-permute-start.8
  19.9 1.2 %collective-permute-done.8 = f32[32,256]{1,0:T(8,128)S(1)} collective-permute-done((f32[32,256]{1,0:T(8,128)S(1)}, f32[32,256]{1,0:T(8,128)S(1)}, u32[]{:S(2)}, u32[]{:S(2)}) %collective-permute-start.8) | collective-permute-done | bytes 32800 | tf_op jit(solution)/shard_map/ppermute | solution.py:260
  21.1 1.6 %collective-permute-start.9 = (f32[32,256]{1,0:T(8,128)S(1)}, f32[32,256]{1,0:T(8,128)S(1)}, u32[]{:S(2)}, u32[]{:S(2)}) collective-permute-start(f32[32,256]{1,0:T(8,128)S(1)} %add.15), channel_id=1, source_target_pairs={{0,2},{1,3},{2,0},{3,1},{4,6},{5,7},{6,4},{7,5},{8,10},{9,11},{10,... | collective-permute-start | bytes 98312 | tf_op jit(solution)/shard_map/ppermute | solution.py:260
  22.7 2.3 %collective-permute-done.9 = f32[32,256]{1,0:T(8,128)S(1)} collective-permute-done((f32[32,256]{1,0:T(8,128)S(1)}, f32[32,256]{1,0:T(8,128)S(1)}, u32[]{:S(2)}, u32[]{:S(2)}) %collective-permute-start.9) | collective-permute-done | bytes 32800 | tf_op jit(solution)/shard_map/ppermute | solution.py:260
  25.0 2.6 %collective-permute-start.10 = (f32[32,256]{1,0:T(8,128)S(1)}, f32[32,256]{1,0:T(8,128)S(1)}, u32[]{:S(2)}, u32[]{:S(2)}) collective-permute-start(f32[32,256]{1,0:T(8,128)S(1)} %add.16), channel_id=1, source_target_pairs={{0,4},{1,5},{2,6},{3,7},{4,0},{5,1},{6,2},{7,3},{8,12},{9,13},{10,... | collective-permute-start | bytes 98312 | tf_op jit(solution)/shard_map/ppermute | solution.py:260
  27.6 2.2 %collective-permute-done.10 = f32[32,256]{1,0:T(8,128)S(1)} collective-permute-done((f32[32,256]{1,0:T(8,128)S(1)}, f32[32,256]{1,0:T(8,128)S(1)}, u32[]{:S(2)}, u32[]{:S(2)}) %collective-permute-start.10) | collective-permute-done | bytes 32800 | tf_op jit(solution)/shard_map/ppermute | solution.py:260
  29.9 1.6 %gram.1 = (f32[4,16,1152]{2,1,0:T(8,128)S(1)}, f32[4,16,1152]{2,1,0:T(8,128)S(1)}) custom-call(f32[256,512]{1,0:T(8,128)S(1)} %copy-done.1, f32[128,512]{1,0:T(8,128)S(1)} %collective-permute-done.refs_1_.refs_3_, f32[128,512]{1,0:T(8,128)S(1)} %collective-permute-done.1.refs_2_.refs_4_, f32[128,512]{1,0:T(8,128)S(1)} %collective-permute-done.3.refs_3_.refs_5_, ...), custom_call_target="tpu_custom_call" | custom-call | flops 1000000 | tf_op jit(solution)/shard_map/gram/pallas_call | solution.py:58
  31.4 0.1 collective-permute-start.11
  31.5 0.7 %collective-permute-start.14 = (f32[1,32,256]{2,1,0:T(8,128)S(1)}, f32[1,32,256]{2,1,0:T(8,128)S(1)}, u32[]{:S(2)}, u32[]{:S(2)}) collective-permute-start(f32[1,32,256]{2,1,0:T(8,128)S(1)} %bitcast.3), channel_id=1, source_target_pairs={{0,8},{8,0},{16,24},{24,16},{1,9},{9,1},{17,25},{25,17},{2,10},{10... | collective-permute-start | bytes 98312 | tf_op jit(solution)/shard_map/ppermute | solution.py:257
  32.2 3.3 %collective-permute-done.14 = f32[1,32,256]{2,1,0:T(8,128)S(1)} collective-permute-done((f32[1,32,256]{2,1,0:T(8,128)S(1)}, f32[1,32,256]{2,1,0:T(8,128)S(1)}, u32[]{:S(2)}, u32[]{:S(2)}) %collective-permute-start.14) | collective-permute-done | bytes 32800 | tf_op jit(solution)/shard_map/ppermute | solution.py:257
  35.5 0.7 %collective-permute-start.15 = (f32[2,32,256]{2,1,0:T(8,128)S(1)}, f32[2,32,256]{2,1,0:T(8,128)S(1)}, u32[]{:S(2)}, u32[]{:S(2)}) collective-permute-start(f32[2,32,256]{2,1,0:T(8,128)S(1)} %pad_maximum_fusion.1), channel_id=1, source_target_pairs={{0,16},{8,24},{16,0},{24,8},{1,17},{9,25},{17,1},{25,9},{2,18},{10... | collective-permute-start | bytes 196616 | tf_op jit(solution)/shard_map/ppermute | solution.py:257
  36.2 1.6 %collective-permute-start.12 = (f32[2,16,1152]{2,1,0:T(8,128)S(1)}, f32[2,16,1152]{2,1,0:T(8,128)S(1)}, u32[]{:S(2)}, u32[]{:S(2)}) collective-permute-start(f32[2,16,1152]{2,1,0:T(8,128)S(1)} %get-tuple-element.26), channel_id=1, source_target_pairs={{0,2},{1,3},{2,0},{3,1},{4,6},{5,7},{6,4},{7,5},{8,10},{9,11},{10,... | collective-permute-start | bytes 442376 | tf_op jit(solution)/shard_map/ppermute | solution.py:260
  37.8 1.9 %collective-permute-done.15 = f32[2,32,256]{2,1,0:T(8,128)S(1)} collective-permute-done((f32[2,32,256]{2,1,0:T(8,128)S(1)}, f32[2,32,256]{2,1,0:T(8,128)S(1)}, u32[]{:S(2)}, u32[]{:S(2)}) %collective-permute-start.15) | collective-permute-done | bytes 65568 | tf_op jit(solution)/shard_map/ppermute | solution.py:257
  39.8 0.1 collective-permute-start.16
  39.8 1.6 %collective-permute-done.12 = f32[2,16,1152]{2,1,0:T(8,128)S(1)} collective-permute-done((f32[2,16,1152]{2,1,0:T(8,128)S(1)}, f32[2,16,1152]{2,1,0:T(8,128)S(1)}, u32[]{:S(2)}, u32[]{:S(2)}) %collective-permute-start.12) | collective-permute-done | bytes 147488 | tf_op jit(solution)/shard_map/ppermute | solution.py:260
  41.4 2.7 %collective-permute-start.13 = (f32[1,16,1152]{2,1,0:T(8,128)S(1)}, f32[1,16,1152]{2,1,0:T(8,128)S(1)}, u32[]{:S(2)}, u32[]{:S(2)}) collective-permute-start(f32[1,16,1152]{2,1,0:T(8,128)S(1)} %get-tuple-element.29), channel_id=1, source_target_pairs={{0,4},{1,5},{2,6},{3,7},{4,0},{5,1},{6,2},{7,3},{8,12},{9,13},{10,... | collective-permute-start | bytes 221192 | tf_op jit(solution)/shard_map/ppermute | solution.py:260
  44.1 4.2 %finish.1 = (f32[64,1024]{1,0:T(8,128)}, f32[16,512]{1,0:T(8,128)}) custom-call(f32[4,32,256]{2,1,0:T(8,128)S(1)} %pad_maximum_fusion.refs_0_, f32[4,32,256]{2,1,0:T(8,128)S(1)} %collective-permute-done.16.refs_1_, f32[256,512]{1,0:T(8,128)S(1)} %copy-done.1, f32[128,512]{1,0:T(8,128)S(1)} %collective-permute-done.refs_1_.refs_3_, ...), custom_call_target="tpu_custom_call" | custom-call | flops 1000000 | tf_op jit(solution)/shard_map/finish/pallas_call | solution.py:58
  48.3 0.7 %unpack.1 = f32[32,1024]{1,0:T(8,128)} custom-call(f32[1,16,1152]{2,1,0:T(8,128)S(1)} %get-tuple-element.30.refs_0_, f32[1,16,1152]{2,1,0:T(8,128)S(1)} %collective-permute-done.13.refs_1_), custom_call_target="tpu_custom_call" | custom-call | flops 1000000 | tf_op jit(solution)/shard_map/unpack/pallas_call | solution.py:58
  (22 shorter events, 0.2 us)
Async XLA Ops:
  0.6 1.0 %copy-start = (f32[256,512]{1,0:T(8,128)S(1)}, f32[256,512]{1,0:T(8,128)}, u32[]{:S(2)}) copy-start(f32[256,512]{1,0:T(8,128)} %refs_2_.1) | copy-start | bytes 1572868
  1.7 0.9 %copy-start.2 = (f32[1024,64]{0,1:T(8,128)S(1)}, f32[1024,64]{0,1:T(8,128)}, u32[]{:S(2)}) copy-start(f32[1024,64]{0,1:T(8,128)} %param.3) | copy-start | bytes 786436
  2.9 7.3 %collective-permute-start.2 = (f32[64,512]{1,0:T(8,128)S(1)}, f32[64,512]{1,0:T(8,128)S(1)}, u32[]{:S(2)}, u32[]{:S(2)}) collective-permute-start(f32[64,512]{1,0:T(8,128)S(1)} %get-tuple-element.18.refs_0_), channel_id=1, source_target_pairs={{0,8},{8,0},{16,24},{24,16},{1,9},{9,1},{17,25},{25,17},{2,10},{10... | collective-permute-start | bytes 393224 | tf_op jit(solution)/shard_map/ppermute | solution.py:257
  5.9 13.5 %copy-start.1 = (f32[256,512]{1,0:T(8,128)S(1)}, f32[256,512]{1,0:T(8,128)}, u32[]{:S(2)}) copy-start(f32[256,512]{1,0:T(8,128)} %refs_2_.1) | copy-start | bytes 1572868
  5.9 9.9 %collective-permute-start = (f32[128,512]{1,0:T(8,128)S(1)}, f32[128,512]{1,0:T(8,128)S(1)}, u32[]{:S(2)}, u32[]{:S(2)}) collective-permute-start(f32[128,512]{1,0:T(8,128)S(1)} %get-tuple-element.16.refs_2_), channel_id=1, source_target_pairs={{0,8},{8,0},{16,24},{24,16},{1,9},{9,1},{17,25},{25,17},{2,10},{10... | collective-permute-start | bytes 786440 | tf_op jit(solution)/shard_map/ppermute | solution.py:257
  6.0 11.9 %collective-permute-start.4 = (f32[128,512]{1,0:T(8,128)S(1)}, f32[128,512]{1,0:T(8,128)S(1)}, u32[]{:S(2)}, u32[]{:S(2)}) collective-permute-start(f32[128,512]{1,0:T(8,128)S(1)} %slice.19), channel_id=1, source_target_pairs={{0,16},{8,24},{16,0},{24,8},{1,17},{9,25},{17,1},{25,9},{2,18},{10... | collective-permute-start | bytes 786440 | tf_op jit(solution)/shard_map/ppermute | solution.py:257
  10.3 9.2 %collective-permute-start.7 = (f32[64,512]{1,0:T(8,128)S(1)}, f32[64,512]{1,0:T(8,128)S(1)}, u32[]{:S(2)}, u32[]{:S(2)}) collective-permute-start(f32[64,512]{1,0:T(8,128)S(1)} %get-tuple-element.20.refs_1_), channel_id=1, source_target_pairs={{0,16},{8,24},{16,0},{24,8},{1,17},{9,25},{17,1},{25,9},{2,18},{10... | collective-permute-start | bytes 393224 | tf_op jit(solution)/shard_map/ppermute | solution.py:257
  12.4 17.4 %collective-permute-start.1 = (f32[128,512]{1,0:T(8,128)S(1)}, f32[128,512]{1,0:T(8,128)S(1)}, u32[]{:S(2)}, u32[]{:S(2)}) collective-permute-start(f32[128,512]{1,0:T(8,128)S(1)} %get-tuple-element.17), channel_id=1, source_target_pairs={{0,8},{8,0},{16,24},{24,16},{1,9},{9,1},{17,25},{25,17},{2,10},{10... | collective-permute-start | bytes 786440 | tf_op jit(solution)/shard_map/ppermute | solution.py:257
  13.9 15.9 %collective-permute-start.3 = (f32[128,512]{1,0:T(8,128)S(1)}, f32[128,512]{1,0:T(8,128)S(1)}, u32[]{:S(2)}, u32[]{:S(2)}) collective-permute-start(f32[128,512]{1,0:T(8,128)S(1)} %get-tuple-element.19), channel_id=1, source_target_pairs={{0,16},{8,24},{16,0},{24,8},{1,17},{9,25},{17,1},{25,9},{2,18},{10... | collective-permute-start | bytes 786440 | tf_op jit(solution)/shard_map/ppermute | solution.py:257
  15.8 14.0 %collective-permute-start.5 = (f32[128,512]{1,0:T(8,128)S(1)}, f32[128,512]{1,0:T(8,128)S(1)}, u32[]{:S(2)}, u32[]{:S(2)}) collective-permute-start(f32[128,512]{1,0:T(8,128)S(1)} %collective-permute-done.refs_1_.refs_3_), channel_id=1, source_target_pairs={{0,16},{8,24},{16,0},{24,8},{1,17},{9,25},{17,1},{25,9},{2,18},{10... | collective-permute-start | bytes 786440 | tf_op jit(solution)/shard_map/ppermute | solution.py:257
  17.9 11.9 %collective-permute-start.6 = (f32[128,512]{1,0:T(8,128)S(1)}, f32[128,512]{1,0:T(8,128)S(1)}, u32[]{:S(2)}, u32[]{:S(2)}) collective-permute-start(f32[128,512]{1,0:T(8,128)S(1)} %collective-permute-done.4.refs_4_.refs_6_), channel_id=1, source_target_pairs={{0,8},{8,0},{16,24},{24,16},{1,9},{9,1},{17,25},{25,17},{2,10},{10... | collective-permute-start | bytes 786440 | tf_op jit(solution)/shard_map/ppermute | solution.py:257
  19.8 1.3 %collective-permute-start.8 = (f32[32,256]{1,0:T(8,128)S(1)}, f32[32,256]{1,0:T(8,128)S(1)}, u32[]{:S(2)}, u32[]{:S(2)}) collective-permute-start(f32[32,256]{1,0:T(8,128)S(1)} %get-tuple-element.22), channel_id=1, source_target_pairs={{0,1},{1,0},{2,3},{3,2},{4,5},{5,4},{6,7},{7,6},{8,9},{9,8},{10,11... | collective-permute-start | bytes 98312 | tf_op jit(solution)/shard_map/ppermute | solution.py:260
  21.1 3.9 %collective-permute-start.9 = (f32[32,256]{1,0:T(8,128)S(1)}, f32[32,256]{1,0:T(8,128)S(1)}, u32[]{:S(2)}, u32[]{:S(2)}) collective-permute-start(f32[32,256]{1,0:T(8,128)S(1)} %add.15), channel_id=1, source_target_pairs={{0,2},{1,3},{2,0},{3,1},{4,6},{5,7},{6,4},{7,5},{8,10},{9,11},{10,... | collective-permute-start | bytes 98312 | tf_op jit(solution)/shard_map/ppermute | solution.py:260
  25.0 4.8 %collective-permute-start.10 = (f32[32,256]{1,0:T(8,128)S(1)}, f32[32,256]{1,0:T(8,128)S(1)}, u32[]{:S(2)}, u32[]{:S(2)}) collective-permute-start(f32[32,256]{1,0:T(8,128)S(1)} %add.16), channel_id=1, source_target_pairs={{0,4},{1,5},{2,6},{3,7},{4,0},{5,1},{6,2},{7,3},{8,12},{9,13},{10,... | collective-permute-start | bytes 98312 | tf_op jit(solution)/shard_map/ppermute | solution.py:260
  31.4 4.7 %collective-permute-start.11 = (f32[4,16,1152]{2,1,0:T(8,128)S(1)}, f32[4,16,1152]{2,1,0:T(8,128)S(1)}, u32[]{:S(2)}, u32[]{:S(2)}) collective-permute-start(f32[4,16,1152]{2,1,0:T(8,128)S(1)} %get-tuple-element.24), channel_id=1, source_target_pairs={{0,1},{1,0},{2,3},{3,2},{4,5},{5,4},{6,7},{7,6},{8,9},{9,8},{10,11... | collective-permute-start | bytes 884744 | tf_op jit(solution)/shard_map/ppermute | solution.py:260
  31.5 4.0 %collective-permute-start.14 = (f32[1,32,256]{2,1,0:T(8,128)S(1)}, f32[1,32,256]{2,1,0:T(8,128)S(1)}, u32[]{:S(2)}, u32[]{:S(2)}) collective-permute-start(f32[1,32,256]{2,1,0:T(8,128)S(1)} %bitcast.3), channel_id=1, source_target_pairs={{0,8},{8,0},{16,24},{24,16},{1,9},{9,1},{17,25},{25,17},{2,10},{10... | collective-permute-start | bytes 98312 | tf_op jit(solution)/shard_map/ppermute | solution.py:257
  35.5 4.3 %collective-permute-start.15 = (f32[2,32,256]{2,1,0:T(8,128)S(1)}, f32[2,32,256]{2,1,0:T(8,128)S(1)}, u32[]{:S(2)}, u32[]{:S(2)}) collective-permute-start(f32[2,32,256]{2,1,0:T(8,128)S(1)} %pad_maximum_fusion.1), channel_id=1, source_target_pairs={{0,16},{8,24},{16,0},{24,8},{1,17},{9,25},{17,1},{25,9},{2,18},{10... | collective-permute-start | bytes 196616 | tf_op jit(solution)/shard_map/ppermute | solution.py:257
  36.2 5.2 %collective-permute-start.12 = (f32[2,16,1152]{2,1,0:T(8,128)S(1)}, f32[2,16,1152]{2,1,0:T(8,128)S(1)}, u32[]{:S(2)}, u32[]{:S(2)}) collective-permute-start(f32[2,16,1152]{2,1,0:T(8,128)S(1)} %get-tuple-element.26), channel_id=1, source_target_pairs={{0,2},{1,3},{2,0},{3,1},{4,6},{5,7},{6,4},{7,5},{8,10},{9,11},{10,... | collective-permute-start | bytes 442376 | tf_op jit(solution)/shard_map/ppermute | solution.py:260
  39.8 4.3 %collective-permute-start.16 = (f32[4,32,256]{2,1,0:T(8,128)S(1)}, f32[4,32,256]{2,1,0:T(8,128)S(1)}, u32[]{:S(2)}, u32[]{:S(2)}) collective-permute-start(f32[4,32,256]{2,1,0:T(8,128)S(1)} %pad_maximum_fusion.refs_0_), channel_id=1, source_target_pairs={{0,1},{1,0},{2,3},{3,2},{4,5},{5,4},{6,7},{7,6},{8,9},{9,8},{10,11... | collective-permute-start | bytes 393224 | tf_op jit(solution)/shard_map/ppermute | solution.py:260
  41.4 6.9 %collective-permute-start.13 = (f32[1,16,1152]{2,1,0:T(8,128)S(1)}, f32[1,16,1152]{2,1,0:T(8,128)S(1)}, u32[]{:S(2)}, u32[]{:S(2)}) collective-permute-start(f32[1,16,1152]{2,1,0:T(8,128)S(1)} %get-tuple-element.29), channel_id=1, source_target_pairs={{0,4},{1,5},{2,6},{3,7},{4,0},{5,1},{6,2},{7,3},{8,12},{9,13},{10,... | collective-permute-start | bytes 221192 | tf_op jit(solution)/shard_map/ppermute | solution.py:260

commit v2 on v1

--- a/solution.py
+++ b/solution.py
@@ -14,7 +14,53 @@
 NT = ((1,), (1,))
 
 
-COST = dict(project=10**6, join=10**6, term=10**10, finish=10**6, gram=10**6, pieces=10**6, unpack=10**6)
+COST = dict(project=10**6, join=10**6, term=10**10, core_sum=10**6, sum=10**6, stack=3 * 10**9, finish=10**10, gram=10**6, pieces=10**6, unpack=10**6)
+
+
+def tree_sum(parts):
+    while len(parts) > 1:
+        paired = [a + b for a, b in zip(parts[::2], parts[1::2])]
+        parts = paired + parts[2 * len(paired) :]
+    return parts[0]
+
+
+def split2(a):
+    hi = a.astype(BF16)
+    return hi, (a - hi.astype(F32)).astype(BF16)
+
+
+def split3(a):
+    hi = a.astype(BF16)
+    rest = a - hi.astype(F32)
+    mid = rest.astype(BF16)
+    return hi, mid, (rest - mid.astype(F32)).astype(BF16)
+
+
+def mm(a, b, dims):
+    return lax.dot_general(a, b, (dims, ((), ())), preferred_element_type=F32)
+
+
+def mm3(a, b, dims):
+    return mm(a[1], b[0], dims) + mm(a[0], b[1], dims) + mm(a[0], b[0], dims)
+
+
+def mm4(a, b):
+    left = jnp.concatenate([a[0], a[0], a[1], a[1]], 1)
+    return mm(left, jnp.concatenate([b[0], b[1], b[0], b[1]], 0), NN)
+
+
+def gram6(a):
+    n = a[0].shape[0]
+    s = jnp.concatenate(a, 0)
+    g = mm(s, s, NT)
+
+    def at(i, j):
+        return g[i * n : (i + 1) * n, j * n : (j + 1) * n]
+
+    return at(0, 0) + ((at(0, 1) + at(1, 0)) + (at(1, 1) + (at(0, 2) + at(2, 0))))
+
+
+COST = dict(project=10**6, join=10**6, term=10**10, core_sum=10**6, sum=10**6, stack=3 * 10**9, finish=10**10, gram=10**6, pieces=10**6, unpack=10**6)
 
 
 def tree_sum(parts):
@@ -90,6 +136,16 @@
     hr = term.shape[0] // 2
     kept_ref[...] = jnp.where(core == 0, term[:hr], term[hr:])
     given_ref[...] = jnp.where(core == 0, term[hr:], term[:hr])
+
+
+def sum_kernel(mine_ref, got_ref, out_ref):
+    out_ref[...] = mine_ref[...] + got_ref[...]
+
+
+def stack_kernel(mine_ref, got_ref, both_ref):
+    n = mine_ref.shape[0]
+    both_ref[:n] = mine_ref[...]
+    both_ref[n:] = got_ref[...]
 
 
 def inverse_factor(inner):
@@ -110,17 +166,21 @@
         for k in range(8):
             pivot = jnp.broadcast_to(cols[k][0][k : k + 1], (8, wide))
             rs = lax.rsqrt(pivot)
-            rs = rs * (1.5 - 0.5 * pivot * rs * rs)
             inv = rs * rs
+            rs = rs * (1.5 - 0.5 * (pivot * inv))
+            inv = inv * (2.0 - pivot * inv)
             row = jnp.broadcast_to(w[b][k : k + 1], (8, wide))
             done.append(row[:1] * rs[:1])
-            m = [a * inv for a in cols[k]]
-            m[0] = jnp.where(sub > k, m[0], F32(0.0))
+            below = [jnp.where(sub > k, cols[k][0], F32(0.0))] + cols[k][1:]
+            m = [a * inv for a in below]
+            for j in range(k + 1, 8):
+                at = jnp.broadcast_to(cols[j][0][k : k + 1], (8, wide))
+                if j == k + 1:
+                    cols[j] = [a - (f * at) * inv for a, f in zip(cols[j], below)]
+                else:
+                    cols[j] = [a - f * at for a, f in zip(cols[j], m)]
             for i in range(b, n // 8):
                 w[i] = w[i] - m[i - b] * row
-            for j in range(k + 1, 8):
-                at = jnp.broadcast_to(cols[j][0][k : k + 1], (8, wide))
-                cols[j] = [a - f * at for a, f in zip(cols[j], m)]
     return jnp.concatenate(done, 0)[:, n : 2 * n]
 
 
@@ -138,7 +198,7 @@
         first, second = jnp.where(core == 0, mine, other), jnp.where(core == 0, other, mine)
         blocks.append(jnp.concatenate([first, second], 0))
     split = [split3(b) for b in blocks]
-    inner = tree_sum([mm6(s, s, NT) for s in split]) * (1.0 / mode)
+    inner = tree_sum([gram6(s) for s in split]) * (1.0 / mode)
     inv = inverse_factor(inner)
     z, at = [], 0
     for s in range(n_row):
@@ -153,10 +213,10 @@
     rank_here = rank // n_row
     for i in range(n_row):
         rows_ref[i] = inv[i * rank_here : (i + 1) * rank_here]
-    core_ref[...] = mm6(split3(rows_ref[row]), split3(z), NN) * (1.0 / math.sqrt(mode))
-    inv3 = split3(inv)
+    core_ref[...] = mm4(split2(rows_ref[row]), split2(z)) * (1.0 / math.sqrt(mode))
+    inv2 = split2(inv)
     for s in range(n_row):
-        block = mm6(inv3, split[s], NN)
+        block = mm4(inv2, split[s])
         if len(nf_ref.shape) == 3:
             nf_ref[row ^ s] = block
         else:
@@ -303,12 +363,47 @@
         work=COST["term"],
         name="term",
     )
-    image = kept + over_col(given, 1)
+    image = call(
+        sum_kernel,
+        jax.ShapeDtypeStruct((hr, rows_here), F32),
+        kept,
+        over_col(given, 1),
+        work=COST["core_sum"],
+        name="core_sum",
+    )
     for s in steps(n_z):
-        image = image + over_col(image, 2 * s)
+        image = call(
+            sum_kernel,
+            jax.ShapeDtypeStruct((hr, rows_here), F32),
+            image,
+            over_col(image, 2 * s),
+            work=COST["sum"],
+            name="z_sum",
+        )
+    given, kept = call(
+        functools.partial(gram_kernel, n_row, n_col, scale, counts),
+        (jax.ShapeDtypeStruct((n_z, half, width), F32),) * 2,
+        *blocks,
+        scratch=[
+            pltpu.VMEM((2 * n_row, group, cols_here), BF16),
+            pltpu.VMEM((2 * n_row, group, cols_here), BF16),
+            pltpu.VMEM((2, 2 * n_row, n_col, half, group), F32),
+        ],
+        after=[image],
+        work=COST["gram"],
+        name="gram",
+    )
     mine = image[None]
     for s in steps(n_row):
-        mine = jnp.concatenate([mine, over_row(mine, s)], 0)
+        mine = call(
+            stack_kernel,
+            jax.ShapeDtypeStruct((2 * s, hr, rows_here), F32),
+            mine,
+            over_row(mine, s),
+            after=[given] if s == 1 else [],
+            work=COST["stack"],
+            name="stack",
+        )
     other = over_col(mine, 1)
 
     rank_here = rank // n_row
@@ -328,19 +423,6 @@
     )
     new_factor = nf.T if whole else nf.transpose(0, 2, 1).reshape(mode, rank)
 
-    given, kept = call(
-        functools.partial(gram_kernel, n_row, n_col, scale, counts),
-        (jax.ShapeDtypeStruct((n_z, half, width), F32),) * 2,
-        *blocks,
-        scratch=[
-            pltpu.VMEM((2 * n_row, group, cols_here), BF16),
-            pltpu.VMEM((2 * n_row, group, cols_here), BF16),
-            pltpu.VMEM((2, 2 * n_row, n_col, half, group), F32),
-        ],
-        after=[image],
-        work=COST["gram"],
-        name="gram",
-    )
     keep, give = call(
         functools.partial(pieces_kernel, n_z),
         (jax.ShapeDtypeStruct((n_z // 2, half, width), F32),) * 2,

time: 49.2 us -> 47.2 us (0.959)
  waiting for transfers between devices: 16.1 us -> 15.1 us
  starting transfers between devices: 22.9 us -> 22.4 us
    ppermute x10, waiting for transfers between devices: 8.82 us -> 7.19 us  [over_row(): return lax.ppermute(x, 'row', [(i, i ^ s) for i in range(n_row)])]
    ppermute x10, starting transfers between devices: 14.2 us -> 12.8 us  [over_row(): return lax.ppermute(x, 'row', [(i, i ^ s) for i in range(n_row)])]
    unnamed x6 -> x4, local copies, waits for them, and re-layouts: 1.99 us -> 0.95 us
    slice x1, local copies, waits for them, and re-layouts: 0.02 us -> 1.03 us  [body(): two_low = over_row(unfolding[group:], 2)]
    ppermute x7, starting transfers between devices: 8.7 us -> 9.55 us  [over_col(): return lax.ppermute(x, 'col', [(i, i ^ s) for i in range(n_col)])]
    ppermute x7, waiting for transfers between devices: 7.32 us -> 7.92 us  [over_col(): return lax.ppermute(x, 'col', [(i, i ^ s) for i in range(n_col)])]
    pallas_call x7 -> x12, Pallas kernels: 7.14 us -> 6.76 us  [call(): pl.pallas_call(run, out_shape=out_shape, in_specs=[pl.BlockSpec(memory_sp...]
  transfers between devices with their start and end apart: 17 -> 17, of which waited for: 8 -> 9; matrix products, arithmetic and copies ran while one was open for 0% -> 0% of each run, Pallas kernels for 9% -> 13%
where the time goes in v2:
time: 47.2 us; the launch traced here: 47 us
  starting transfers between devices  22.4 us (47%)
  waiting for transfers between devices  15.1 us (32%)
  Pallas kernels  6.76 us (14%)
  local copies, waits for them, and re-layouts  1.99 us (4%)
  between operations  0.73 us (2%)
    ppermute x10, starting transfers between devices, over_row(): return lax.ppermute(x, 'row', [(i, i ^ s) for i in range(n_row)])  12.8 us
    ppermute x7, starting transfers between devices, over_col(): return lax.ppermute(x, 'col', [(i, i ^ s) for i in range(n_col)])  9.55 us
    ppermute x7, waiting for transfers between devices, over_col(): return lax.ppermute(x, 'col', [(i, i ^ s) for i in range(n_col)])  7.92 us
    ppermute x10, waiting for transfers between devices, over_row(): return lax.ppermute(x, 'row', [(i, i ^ s) for i in range(n_row)])  7.19 us
    pallas_call x12, Pallas kernels, call(): pl.pallas_call(run, out_shape=out_shape, in_specs=[pl.BlockSpec(memory_sp...  6.76 us
    slice x1, local copies, waits for them, and re-layouts, body(): two_low = over_row(unfolding[group:], 2)  1.03 us
    unnamed x4, local copies, waits for them, and re-layouts  0.95 us
  transfers between devices with their start and end apart: 17, of which 9 were waited for; matrix products, arithmetic and copies ran while one was open for 0% of the time, Pallas kernels for 13%

profile of v2, /device:TPU:0, one launch (start us, length us, event | category | flops | bytes accessed | tf_op | source)
XLA Modules:
  0.0 47.0 jit_solution(14415850408335131103)
XLA Ops:
  0.6 1.0 %slice.19 = f32[128,512]{1,0:T(8,128)S(1)} slice(f32[256,512]{1,0:T(8,128)} %refs_2_.1), slice={[128:256], [0:512]} | slice | bytes 524288 | tf_op jit(solution)/shard_map/slice | solution.py:329
  1.7 3.0 %collective-permute-start.4 = (f32[128,512]{1,0:T(8,128)S(1)}, f32[128,512]{1,0:T(8,128)S(1)}, u32[]{:S(2)}, u32[]{:S(2)}) collective-permute-start(f32[128,512]{1,0:T(8,128)S(1)} %slice.19), channel_id=1, source_target_pairs={{0,16},{8,24},{16,0},{24,8},{1,17},{9,25},{17,1},{25,9},{2,18},{10... | collective-permute-start | bytes 786440 | tf_op jit(solution)/shard_map/ppermute | solution.py:317
  4.7 0.9 %copy-done.1 = f32[1024,64]{0,1:T(8,128)S(1)} copy-done((f32[1024,64]{0,1:T(8,128)S(1)}, f32[1024,64]{0,1:T(8,128)}, u32[]{:S(2)}) %copy-start.1) | copy-done | bytes 262168
  5.7 0.3 project.1
  5.9 1.6 %collective-permute-start.2 = (f32[64,512]{1,0:T(8,128)S(1)}, f32[64,512]{1,0:T(8,128)S(1)}, u32[]{:S(2)}, u32[]{:S(2)}) collective-permute-start(f32[64,512]{1,0:T(8,128)S(1)} %get-tuple-element.18.refs_0_), channel_id=1, source_target_pairs={{0,8},{8,0},{16,24},{24,16},{1,9},{9,1},{17,25},{25,17},{2,10},{10... | collective-permute-start | bytes 393224 | tf_op jit(solution)/shard_map/ppermute | solution.py:317
  7.5 0.5 %collective-permute-start = (f32[128,512]{1,0:T(8,128)S(1)}, f32[128,512]{1,0:T(8,128)S(1)}, u32[]{:S(2)}, u32[]{:S(2)}) collective-permute-start(f32[128,512]{1,0:T(8,128)S(1)} %get-tuple-element.16.refs_2_), channel_id=1, source_target_pairs={{0,8},{8,0},{16,24},{24,16},{1,9},{9,1},{17,25},{25,17},{2,10},{10... | collective-permute-start | bytes 786440 | tf_op jit(solution)/shard_map/ppermute | solution.py:317
  8.0 4.4 %collective-permute-done.2.refs_1_ = f32[64,512]{1,0:T(8,128)S(1)} collective-permute-done((f32[64,512]{1,0:T(8,128)S(1)}, f32[64,512]{1,0:T(8,128)S(1)}, u32[]{:S(2)}, u32[]{:S(2)}) %collective-permute-start.2) | collective-permute-done | bytes 131104 | tf_op jit(solution)/shard_map/ppermute | solution.py:317
  12.5 0.1 collective-permute-start.7
  12.5 2.0 %collective-permute-start.1 = (f32[128,512]{1,0:T(8,128)S(1)}, f32[128,512]{1,0:T(8,128)S(1)}, u32[]{:S(2)}, u32[]{:S(2)}) collective-permute-start(f32[128,512]{1,0:T(8,128)S(1)} %get-tuple-element.17), channel_id=1, source_target_pairs={{0,8},{8,0},{16,24},{24,16},{1,9},{9,1},{17,25},{25,17},{2,10},{10... | collective-permute-start | bytes 786440 | tf_op jit(solution)/shard_map/ppermute | solution.py:317
  14.5 1.5 %collective-permute-start.3 = (f32[128,512]{1,0:T(8,128)S(1)}, f32[128,512]{1,0:T(8,128)S(1)}, u32[]{:S(2)}, u32[]{:S(2)}) collective-permute-start(f32[128,512]{1,0:T(8,128)S(1)} %get-tuple-element.19), channel_id=1, source_target_pairs={{0,16},{8,24},{16,0},{24,8},{1,17},{9,25},{17,1},{25,9},{2,18},{10... | collective-permute-start | bytes 786440 | tf_op jit(solution)/shard_map/ppermute | solution.py:317
  16.0 0.5 %collective-permute-start.6 = (f32[128,512]{1,0:T(8,128)S(1)}, f32[128,512]{1,0:T(8,128)S(1)}, u32[]{:S(2)}, u32[]{:S(2)}) collective-permute-start(f32[128,512]{1,0:T(8,128)S(1)} %collective-permute-done.4.refs_4_.refs_6_), channel_id=1, source_target_pairs={{0,8},{8,0},{16,24},{24,16},{1,9},{9,1},{17,25},{25,17},{2,10},{10... | collective-permute-start | bytes 786440 | tf_op jit(solution)/shard_map/ppermute | solution.py:317
  16.6 1.5 %collective-permute-done.refs_1_.refs_3_ = f32[128,512]{1,0:T(8,128)S(1)} collective-permute-done((f32[128,512]{1,0:T(8,128)S(1)}, f32[128,512]{1,0:T(8,128)S(1)}, u32[]{:S(2)}, u32[]{:S(2)}) %collective-permute-start) | collective-permute-done | bytes 262176 | tf_op jit(solution)/shard_map/ppermute | solution.py:317
  18.0 0.1 collective-permute-done.7.refs_2_
  18.1 0.4 term.1
  18.5 0.1 collective-permute-start.8
  18.6 1.2 %collective-permute-done.8.refs_1_ = f32[32,256]{1,0:T(8,128)S(1)} collective-permute-done((f32[32,256]{1,0:T(8,128)S(1)}, f32[32,256]{1,0:T(8,128)S(1)}, u32[]{:S(2)}, u32[]{:S(2)}) %collective-permute-start.8) | collective-permute-done | bytes 32800 | tf_op jit(solution)/shard_map/ppermute | solution.py:320
  19.8 2.0 %collective-permute-start.9 = (f32[32,256]{1,0:T(8,128)S(1)}, f32[32,256]{1,0:T(8,128)S(1)}, u32[]{:S(2)}, u32[]{:S(2)}) collective-permute-start(f32[32,256]{1,0:T(8,128)S(1)} %core_sum.1.refs_0_), channel_id=1, source_target_pairs={{0,2},{1,3},{2,0},{3,1},{4,6},{5,7},{6,4},{7,5},{8,10},{9,11},{10,... | collective-permute-start | bytes 98312 | tf_op jit(solution)/shard_map/ppermute | solution.py:320
  21.8 1.9 %collective-permute-done.9.refs_1_ = f32[32,256]{1,0:T(8,128)S(1)} collective-permute-done((f32[32,256]{1,0:T(8,128)S(1)}, f32[32,256]{1,0:T(8,128)S(1)}, u32[]{:S(2)}, u32[]{:S(2)}) %collective-permute-start.9) | collective-permute-done | bytes 32800 | tf_op jit(solution)/shard_map/ppermute | solution.py:320
  23.7 3.0 %collective-permute-start.10 = (f32[32,256]{1,0:T(8,128)S(1)}, f32[32,256]{1,0:T(8,128)S(1)}, u32[]{:S(2)}, u32[]{:S(2)}) collective-permute-start(f32[32,256]{1,0:T(8,128)S(1)} %z_sum.2.refs_0_), channel_id=1, source_target_pairs={{0,4},{1,5},{2,6},{3,7},{4,0},{5,1},{6,2},{7,3},{8,12},{9,13},{10,... | collective-permute-start | bytes 98312 | tf_op jit(solution)/shard_map/ppermute | solution.py:320
  26.7 1.9 %collective-permute-done.10.refs_1_ = f32[32,256]{1,0:T(8,128)S(1)} collective-permute-done((f32[32,256]{1,0:T(8,128)S(1)}, f32[32,256]{1,0:T(8,128)S(1)}, u32[]{:S(2)}, u32[]{:S(2)}) %collective-permute-start.10) | collective-permute-done | bytes 32800 | tf_op jit(solution)/shard_map/ppermute | solution.py:320
  28.6 1.8 %collective-permute-start.14 = (f32[1,32,256]{2,1,0:T(8,128)S(1)}, f32[1,32,256]{2,1,0:T(8,128)S(1)}, u32[]{:S(2)}, u32[]{:S(2)}) collective-permute-start(f32[1,32,256]{2,1,0:T(8,128)S(1)} %bitcast.4), channel_id=1, source_target_pairs={{0,8},{8,0},{16,24},{24,16},{1,9},{9,1},{17,25},{25,17},{2,10},{10... | collective-permute-start | bytes 98312 | tf_op jit(solution)/shard_map/ppermute | solution.py:317
  30.4 1.6 %gram.1 = (f32[4,16,1152]{2,1,0:T(8,128)S(1)}, f32[4,16,1152]{2,1,0:T(8,128)S(1)}) custom-call(f32[256,512]{1,0:T(8,128)S(1)} %copy-done, f32[128,512]{1,0:T(8,128)S(1)} %collective-permute-done.refs_1_.refs_3_, f32[128,512]{1,0:T(8,128)S(1)} %collective-permute-done.1.refs_2_.refs_4_, f32[128,512]{1,0:T(8,128)S(1)} %collective-permute-done.3.refs_3_.refs_5_, ...), custom_call_target="tpu_custom_call" | custom-call | flops 1000000 | tf_op jit(solution)/shard_map/gram/pallas_call | solution.py:104
  32.0 0.1 collective-permute-start.11
  32.1 0.5 collective-permute-done.14.refs_1_
  32.6 1.8 %collective-permute-start.15 = (f32[2,32,256]{2,1,0:T(8,128)S(1)}, f32[2,32,256]{2,1,0:T(8,128)S(1)}, u32[]{:S(2)}, u32[]{:S(2)}) collective-permute-start(f32[2,32,256]{2,1,0:T(8,128)S(1)} %stack.2.refs_0_), channel_id=1, source_target_pairs={{0,16},{8,24},{16,0},{24,8},{1,17},{9,25},{17,1},{25,9},{2,18},{10... | collective-permute-start | bytes 196616 | tf_op jit(solution)/shard_map/ppermute | solution.py:317
  34.4 1.6 %collective-permute-start.12 = (f32[2,16,1152]{2,1,0:T(8,128)S(1)}, f32[2,16,1152]{2,1,0:T(8,128)S(1)}, u32[]{:S(2)}, u32[]{:S(2)}) collective-permute-start(f32[2,16,1152]{2,1,0:T(8,128)S(1)} %get-tuple-element.26), channel_id=1, source_target_pairs={{0,2},{1,3},{2,0},{3,1},{4,6},{5,7},{6,4},{7,5},{8,10},{9,11},{10,... | collective-permute-start | bytes 442376 | tf_op jit(solution)/shard_map/ppermute | solution.py:320
  36.1 0.8 %collective-permute-done.15.refs_1_ = f32[2,32,256]{2,1,0:T(8,128)S(1)} collective-permute-done((f32[2,32,256]{2,1,0:T(8,128)S(1)}, f32[2,32,256]{2,1,0:T(8,128)S(1)}, u32[]{:S(2)}, u32[]{:S(2)}) %collective-permute-start.15) | collective-permute-done | bytes 65568 | tf_op jit(solution)/shard_map/ppermute | solution.py:317
  36.8 0.1 collective-permute-start.16
  36.9 2.9 %collective-permute-done.12 = f32[2,16,1152]{2,1,0:T(8,128)S(1)} collective-permute-done((f32[2,16,1152]{2,1,0:T(8,128)S(1)}, f32[2,16,1152]{2,1,0:T(8,128)S(1)}, u32[]{:S(2)}, u32[]{:S(2)}) %collective-permute-start.12) | collective-permute-done | bytes 147488 | tf_op jit(solution)/shard_map/ppermute | solution.py:320
  39.8 2.7 %collective-permute-start.13 = (f32[1,16,1152]{2,1,0:T(8,128)S(1)}, f32[1,16,1152]{2,1,0:T(8,128)S(1)}, u32[]{:S(2)}, u32[]{:S(2)}) collective-permute-start(f32[1,16,1152]{2,1,0:T(8,128)S(1)} %get-tuple-element.29), channel_id=1, source_target_pairs={{0,4},{1,5},{2,6},{3,7},{4,0},{5,1},{6,2},{7,3},{8,12},{9,13},{10,... | collective-permute-start | bytes 221192 | tf_op jit(solution)/shard_map/ppermute | solution.py:320
  42.5 3.8 %finish.1 = (f32[64,1024]{1,0:T(8,128)}, f32[16,512]{1,0:T(8,128)}) custom-call(f32[4,32,256]{2,1,0:T(8,128)S(1)} %stack.3.refs_0_, f32[4,32,256]{2,1,0:T(8,128)S(1)} %collective-permute-done.16.refs_1_, f32[256,512]{1,0:T(8,128)S(1)} %copy-done, f32[128,512]{1,0:T(8,128)S(1)} %collective-permute-done.refs_1_.refs_3_, ...), custom_call_target="tpu_custom_call" | custom-call | flops 10000000000 | tf_op jit(solution)/shard_map/finish/pallas_call | solution.py:104
  46.3 0.7 %unpack.1 = f32[32,1024]{1,0:T(8,128)} custom-call(f32[1,16,1152]{2,1,0:T(8,128)S(1)} %get-tuple-element.30.refs_0_, f32[1,16,1152]{2,1,0:T(8,128)S(1)} %collective-permute-done.13.refs_1_), custom_call_target="tpu_custom_call" | custom-call | flops 1000000 | tf_op jit(solution)/shard_map/unpack/pallas_call | solution.py:104
  (20 shorter events, 0.1 us)
Async XLA Ops:
  0.6 4.1 %copy-start = (f32[256,512]{1,0:T(8,128)S(1)}, f32[256,512]{1,0:T(8,128)}, u32[]{:S(2)}) copy-start(f32[256,512]{1,0:T(8,128)} %refs_2_.1) | copy-start | bytes 1572868
  1.7 14.4 %collective-permute-start.4 = (f32[128,512]{1,0:T(8,128)S(1)}, f32[128,512]{1,0:T(8,128)S(1)}, u32[]{:S(2)}, u32[]{:S(2)}) collective-permute-start(f32[128,512]{1,0:T(8,128)S(1)} %slice.19), channel_id=1, source_target_pairs={{0,16},{8,24},{16,0},{24,8},{1,17},{9,25},{17,1},{25,9},{2,18},{10... | collective-permute-start | bytes 786440 | tf_op jit(solution)/shard_map/ppermute | solution.py:317
  4.7 1.0 %copy-start.1 = (f32[1024,64]{0,1:T(8,128)S(1)}, f32[1024,64]{0,1:T(8,128)}, u32[]{:S(2)}) copy-start(f32[1024,64]{0,1:T(8,128)} %param.3) | copy-start | bytes 786436
  5.9 6.5 %collective-permute-start.2 = (f32[64,512]{1,0:T(8,128)S(1)}, f32[64,512]{1,0:T(8,128)S(1)}, u32[]{:S(2)}, u32[]{:S(2)}) collective-permute-start(f32[64,512]{1,0:T(8,128)S(1)} %get-tuple-element.18.refs_0_), channel_id=1, source_target_pairs={{0,8},{8,0},{16,24},{24,16},{1,9},{9,1},{17,25},{25,17},{2,10},{10... | collective-permute-start | bytes 393224 | tf_op jit(solution)/shard_map/ppermute | solution.py:317
  7.5 10.5 %collective-permute-start = (f32[128,512]{1,0:T(8,128)S(1)}, f32[128,512]{1,0:T(8,128)S(1)}, u32[]{:S(2)}, u32[]{:S(2)}) collective-permute-start(f32[128,512]{1,0:T(8,128)S(1)} %get-tuple-element.16.refs_2_), channel_id=1, source_target_pairs={{0,8},{8,0},{16,24},{24,16},{1,9},{9,1},{17,25},{25,17},{2,10},{10... | collective-permute-start | bytes 786440 | tf_op jit(solution)/shard_map/ppermute | solution.py:317
  12.5 5.7 %collective-permute-start.7 = (f32[64,512]{1,0:T(8,128)S(1)}, f32[64,512]{1,0:T(8,128)S(1)}, u32[]{:S(2)}, u32[]{:S(2)}) collective-permute-start(f32[64,512]{1,0:T(8,128)S(1)} %get-tuple-element.20.refs_1_), channel_id=1, source_target_pairs={{0,16},{8,24},{16,0},{24,8},{1,17},{9,25},{17,1},{25,9},{2,18},{10... | collective-permute-start | bytes 393224 | tf_op jit(solution)/shard_map/ppermute | solution.py:317
  12.5 17.9 %collective-permute-start.1 = (f32[128,512]{1,0:T(8,128)S(1)}, f32[128,512]{1,0:T(8,128)S(1)}, u32[]{:S(2)}, u32[]{:S(2)}) collective-permute-start(f32[128,512]{1,0:T(8,128)S(1)} %get-tuple-element.17), channel_id=1, source_target_pairs={{0,8},{8,0},{16,24},{24,16},{1,9},{9,1},{17,25},{25,17},{2,10},{10... | collective-permute-start | bytes 786440 | tf_op jit(solution)/shard_map/ppermute | solution.py:317
  14.5 15.9 %collective-permute-start.3 = (f32[128,512]{1,0:T(8,128)S(1)}, f32[128,512]{1,0:T(8,128)S(1)}, u32[]{:S(2)}, u32[]{:S(2)}) collective-permute-start(f32[128,512]{1,0:T(8,128)S(1)} %get-tuple-element.19), channel_id=1, source_target_pairs={{0,16},{8,24},{16,0},{24,8},{1,17},{9,25},{17,1},{25,9},{2,18},{10... | collective-permute-start | bytes 786440 | tf_op jit(solution)/shard_map/ppermute | solution.py:317
  16.0 14.4 %collective-permute-start.6 = (f32[128,512]{1,0:T(8,128)S(1)}, f32[128,512]{1,0:T(8,128)S(1)}, u32[]{:S(2)}, u32[]{:S(2)}) collective-permute-start(f32[128,512]{1,0:T(8,128)S(1)} %collective-permute-done.4.refs_4_.refs_6_), channel_id=1, source_target_pairs={{0,8},{8,0},{16,24},{24,16},{1,9},{9,1},{17,25},{25,17},{2,10},{10... | collective-permute-start | bytes 786440 | tf_op jit(solution)/shard_map/ppermute | solution.py:317
  18.0 12.4 %collective-permute-start.5 = (f32[128,512]{1,0:T(8,128)S(1)}, f32[128,512]{1,0:T(8,128)S(1)}, u32[]{:S(2)}, u32[]{:S(2)}) collective-permute-start(f32[128,512]{1,0:T(8,128)S(1)} %collective-permute-done.refs_1_.refs_3_), channel_id=1, source_target_pairs={{0,16},{8,24},{16,0},{24,8},{1,17},{9,25},{17,1},{25,9},{2,18},{10... | collective-permute-start | bytes 786440 | tf_op jit(solution)/shard_map/ppermute | solution.py:317
  18.5 1.3 %collective-permute-start.8 = (f32[32,256]{1,0:T(8,128)S(1)}, f32[32,256]{1,0:T(8,128)S(1)}, u32[]{:S(2)}, u32[]{:S(2)}) collective-permute-start(f32[32,256]{1,0:T(8,128)S(1)} %get-tuple-element.22), channel_id=1, source_target_pairs={{0,1},{1,0},{2,3},{3,2},{4,5},{5,4},{6,7},{7,6},{8,9},{9,8},{10,11... | collective-permute-start | bytes 98312 | tf_op jit(solution)/shard_map/ppermute | solution.py:320
  19.8 3.9 %collective-permute-start.9 = (f32[32,256]{1,0:T(8,128)S(1)}, f32[32,256]{1,0:T(8,128)S(1)}, u32[]{:S(2)}, u32[]{:S(2)}) collective-permute-start(f32[32,256]{1,0:T(8,128)S(1)} %core_sum.1.refs_0_), channel_id=1, source_target_pairs={{0,2},{1,3},{2,0},{3,1},{4,6},{5,7},{6,4},{7,5},{8,10},{9,11},{10,... | collective-permute-start | bytes 98312 | tf_op jit(solution)/shard_map/ppermute | solution.py:320
  23.7 4.9 %collective-permute-start.10 = (f32[32,256]{1,0:T(8,128)S(1)}, f32[32,256]{1,0:T(8,128)S(1)}, u32[]{:S(2)}, u32[]{:S(2)}) collective-permute-start(f32[32,256]{1,0:T(8,128)S(1)} %z_sum.2.refs_0_), channel_id=1, source_target_pairs={{0,4},{1,5},{2,6},{3,7},{4,0},{5,1},{6,2},{7,3},{8,12},{9,13},{10,... | collective-permute-start | bytes 98312 | tf_op jit(solution)/shard_map/ppermute | solution.py:320
  28.6 3.9 %collective-permute-start.14 = (f32[1,32,256]{2,1,0:T(8,128)S(1)}, f32[1,32,256]{2,1,0:T(8,128)S(1)}, u32[]{:S(2)}, u32[]{:S(2)}) collective-permute-start(f32[1,32,256]{2,1,0:T(8,128)S(1)} %bitcast.4), channel_id=1, source_target_pairs={{0,8},{8,0},{16,24},{24,16},{1,9},{9,1},{17,25},{25,17},{2,10},{10... | collective-permute-start | bytes 98312 | tf_op jit(solution)/shard_map/ppermute | solution.py:317
  32.0 2.4 %collective-permute-start.11 = (f32[4,16,1152]{2,1,0:T(8,128)S(1)}, f32[4,16,1152]{2,1,0:T(8,128)S(1)}, u32[]{:S(2)}, u32[]{:S(2)}) collective-permute-start(f32[4,16,1152]{2,1,0:T(8,128)S(1)} %get-tuple-element.24.refs_2_), channel_id=1, source_target_pairs={{0,1},{1,0},{2,3},{3,2},{4,5},{5,4},{6,7},{7,6},{8,9},{9,8},{10,11... | collective-permute-start | bytes 884744 | tf_op jit(solution)/shard_map/ppermute | solution.py:320
  32.6 4.3 %collective-permute-start.15 = (f32[2,32,256]{2,1,0:T(8,128)S(1)}, f32[2,32,256]{2,1,0:T(8,128)S(1)}, u32[]{:S(2)}, u32[]{:S(2)}) collective-permute-start(f32[2,32,256]{2,1,0:T(8,128)S(1)} %stack.2.refs_0_), channel_id=1, source_target_pairs={{0,16},{8,24},{16,0},{24,8},{1,17},{9,25},{17,1},{25,9},{2,18},{10... | collective-permute-start | bytes 196616 | tf_op jit(solution)/shard_map/ppermute | solution.py:317
  34.4 5.4 %collective-permute-start.12 = (f32[2,16,1152]{2,1,0:T(8,128)S(1)}, f32[2,16,1152]{2,1,0:T(8,128)S(1)}, u32[]{:S(2)}, u32[]{:S(2)}) collective-permute-start(f32[2,16,1152]{2,1,0:T(8,128)S(1)} %get-tuple-element.26), channel_id=1, source_target_pairs={{0,2},{1,3},{2,0},{3,1},{4,6},{5,7},{6,4},{7,5},{8,10},{9,11},{10,... | collective-permute-start | bytes 442376 | tf_op jit(solution)/shard_map/ppermute | solution.py:320
  36.8 5.7 %collective-permute-start.16 = (f32[4,32,256]{2,1,0:T(8,128)S(1)}, f32[4,32,256]{2,1,0:T(8,128)S(1)}, u32[]{:S(2)}, u32[]{:S(2)}) collective-permute-start(f32[4,32,256]{2,1,0:T(8,128)S(1)} %stack.3.refs_0_), channel_id=1, source_target_pairs={{0,1},{1,0},{2,3},{3,2},{4,5},{5,4},{6,7},{7,6},{8,9},{9,8},{10,11... | collective-permute-start | bytes 393224 | tf_op jit(solution)/shard_map/ppermute | solution.py:320
  39.8 6.5 %collective-permute-start.13 = (f32[1,16,1152]{2,1,0:T(8,128)S(1)}, f32[1,16,1152]{2,1,0:T(8,128)S(1)}, u32[]{:S(2)}, u32[]{:S(2)}) collective-permute-start(f32[1,16,1152]{2,1,0:T(8,128)S(1)} %get-tuple-element.29), channel_id=1, source_target_pairs={{0,4},{1,5},{2,6},{3,7},{4,0},{5,1},{6,2},{7,3},{8,12},{9,13},{10,... | collective-permute-start | bytes 221192 | tf_op jit(solution)/shard_map/ppermute | solution.py:320
